TPU v7x, 512 devices: a whole 4x4x16 slice. The times are simulated.
512 devices in a mesh: gx: 4 (over x), gy: 8 (over y, core), gz: 16 (over z).
Axes of the slice: x: 4, y: 4, z: 16, core: 2. Of those that a mesh axis runs over, the one named last changes fastest.
Arguments:
- volume: bfloat16 [2048, 512, 512], P('gz', 'gy', 'gx'), may hold values from -6 to 6
- tf_color: float32 [3, 16], replicated, may hold values from 0 to 1
- tf_opacity: float32 [16], replicated, may hold values from 0.0005 to 0.008
- active: int32 [256, 8, 4], P('gz', 'gy', 'gx'), may hold values from 0 to 1, as said below
Outputs:
- composited: float32 [4, 512, 768], P(None, ('gx', 'gy', 'gz'))
Inputs may be any that keep to these rules, and one draw needn't show every extreme that they name: `active`: the 16 bricks of each block (one gy, gx index and 16 consecutive entries along the first dimension) hold at least one 1; in every draw some block has all 16 set.
All inputs are finite; a program needn't handle non-finite values.
Results may differ from a plain program's by a relative error of at most 0.0014.
Values may be sent and summed in bfloat16 or wider, within the bound.
No kernel may reach another device: no remote copies, remote signals or barrier semaphores. Data moves between devices by JAX's collectives and lax.ppermute only.
A program may use at most 64 MiB of HBM per device.

v0:
```python
import jax
import jax.numpy as jnp
from jax import lax
from jax.sharding import PartitionSpec as P

BZ = 8


LIMIT = 3.0


def from_behind(block, axis, distance):
    devices = range(lax.axis_size(axis))
    route = [(i - distance, i) for i in devices if i - distance in devices]
    return lax.ppermute(block, axis, route)


def partner(value, axis, bit):
    return lax.ppermute(value, axis, [(i, i ^ 1 << bit) for i in range(lax.axis_size(axis))])


def classify(values, tf_color, tf_opacity):
    knot_count = tf_opacity.shape[0]
    spacing = 2.0 * LIMIT / (knot_count - 1)
    opacity = jnp.zeros(values.shape, jnp.float32)
    shades = [jnp.zeros(values.shape, jnp.float32) for channel in range(3)]
    for knot_index in range(knot_count):
        centre = -LIMIT + knot_index * spacing
        weight = jnp.maximum(0.0, 1.0 - jnp.abs(values - centre) / spacing)
        opacity = opacity + weight * tf_opacity[knot_index]
        shades = [shades[channel] + weight * tf_color[channel, knot_index] for channel in range(3)]
    return jnp.stack([shades[0] * opacity, shades[1] * opacity, shades[2] * opacity, opacity])


def composite(nearer, farther):
    return nearer + (1.0 - nearer[3:4]) * farther


def render_brick(cell_values, rim_cells, tf_color, tf_opacity):
    layers = cell_values.shape[0]
    classified = classify(cell_values.astype(jnp.float32), tf_color, tf_opacity)
    edge = classify(rim_cells.astype(jnp.float32), tf_color, tf_opacity)
    running = jnp.zeros((4,) + cell_values.shape[1:], jnp.float32)
    for layer_index in range(layers):
        fraction = layer_index / layers
        current = classified[:, layer_index]
        shifted = jnp.concatenate([edge[:, layer_index, :, None], current[:, :, :-1]], axis=2)
        sample = (1.0 - fraction) * current + fraction * shifted
        running = composite(running, sample)
    return running


def render_marked(cell_stack, rim_stack, mark_stack, threshold, tf_color, tf_opacity):
    blank_shape = (4,) + cell_stack.shape[2:]

    def render_one(inputs):
        cell_values, rim_cells, brick_mark = inputs

        def render_now():
            return render_brick(cell_values, rim_cells, tf_color, tf_opacity)

        def render_none():
            return jnp.zeros(blank_shape, jnp.float32)

        return lax.cond(brick_mark > threshold, render_now, render_none)

    return lax.map(render_one, (cell_stack, rim_stack, mark_stack))


def block_window(images):
    brick_count, channels, row_count, col_count = images.shape
    window = jnp.zeros((channels, row_count, col_count + brick_count), jnp.float32)

    def place_brick(brick_index, window):
        covered = lax.dynamic_slice_in_dim(window, brick_index, col_count, 2)
        merged = composite(covered, images[brick_index])
        return lax.dynamic_update_slice_in_dim(window, merged, brick_index, 2)

    return lax.fori_loop(0, brick_count, place_brick, window)


def split_lowest(current, my_bit):
    groups = current.reshape(current.shape[0], current.shape[1] // 2, 2, current.shape[2])
    kept = jnp.where(my_bit == 0, groups[:, :, 0], groups[:, :, 1])
    handed = jnp.where(my_bit == 0, groups[:, :, 1], groups[:, :, 0])
    return (kept, handed)


def join_pair(kept, arrived, kept_front):
    return jnp.where(kept_front, composite(kept, arrived), composite(arrived, kept))


def body(volume, tf_color, tf_opacity, active):
    layer_total, row_count, col_count = volume.shape
    brick_count = layer_total // BZ
    bricks = volume.reshape(brick_count, BZ, row_count, col_count)
    rim_all = from_behind(volume[:, :, col_count - 1], "gx", 1)
    rim_layers = rim_all.reshape(brick_count, BZ, row_count)
    brick_flags = active.reshape(brick_count)
    images = render_marked(bricks, rim_layers, brick_flags, 0, tf_color, tf_opacity)
    window = block_window(images)
    across_count = lax.axis_size("gx")
    down_count = lax.axis_size("gy")
    depth_count = lax.axis_size("gz")
    height = row_count * down_count
    breadth = col_count * across_count + brick_count * depth_count
    devices_all = across_count * down_count * depth_count
    column_start = lax.axis_index("gx") * col_count + lax.axis_index("gz") * brick_count
    picture = jnp.zeros((4, height, breadth), jnp.float32)
    corner = (jnp.int32(0), lax.axis_index("gy") * row_count, column_start)
    picture = lax.dynamic_update_slice(picture, window, corner)
    held = height * breadth // devices_all
    current = jnp.transpose(picture.reshape(4, held, devices_all), (0, 2, 1))
    for bit_index in range(depth_count.bit_length() - 1):
        my_bit = lax.axis_index("gz") >> bit_index & 1
        kept, handed = split_lowest(current, my_bit)
        arrived = partner(handed, "gz", bit_index)
        current = join_pair(kept, arrived, my_bit == 0)
    for bit_index in range(down_count.bit_length() - 1):
        my_bit = lax.axis_index("gy") >> bit_index & 1
        kept, handed = split_lowest(current, my_bit)
        arrived = partner(handed, "gy", bit_index)
        current = join_pair(kept, arrived, my_bit == 0)
    for bit_index in range(across_count.bit_length() - 1):
        my_bit = lax.axis_index("gx") >> bit_index & 1
        kept, handed = split_lowest(current, my_bit)
        arrived = partner(handed, "gx", bit_index)
        current = join_pair(kept, arrived, my_bit == 1)
    return current


def solution(mesh):
    placed = (P("gz", "gy", "gx"), P(), P(), P("gz", "gy", "gx"))
    return jax.shard_map(
        body,
        mesh=mesh,
        in_specs=placed,
        out_specs=P(None, ("gx", "gy", "gz"), None),
        check_vma=False,
    )
```

profile of v0, /device:TPU:1, one launch (start us, length us, event | category | flops | bytes accessed | tf_op | source)
XLA Modules:
  0.0 1758.4 jit_solution(5399676217031434721)
XLA Ops:
  9.4 396.3 %while.23 = (s32[]{:T(128)}, f32[16,4,64,128]{3,2,1,0:T(8,128)}, s32[16]{0:T(128)S(1)}, bf16[16,8,64,128]{3,2,1,0:T(8,128)(2,1)}, f32[3,16]{1,0:T(4,128)S(1)}, /...) while((s32[]{:T(128)}, f32[16,4,64,128]{3,2,1,0:T(8,128)}, s32[16]{0:T(128)S(1)}, ...), condition=%wide.region_3.4_spmd, body=%wide.region_0.3_spmd.sunk | while | flops 27769860 | bytes 15819699 | solution.py:67
  18.4 91.4 %conditional.2 = (f32[1,4,64,128]{3,2,1,0:T(8,128)S(1)}) conditional(s32[]{:T(128)} %bitcast.339, () %tuple.167, (bf16[16,8,64,128]{3,2,1,0:T(8,128)(2,1)}, s32[]{:T(128)}, f32[3,16]{1,0:T(4,128)S(1)}, f32[16]{0:T(128)S(1)}, bf16[16,8,64]{2,1,0:T(8,128)(2,1)S(1)}) %tuple.168), branch_computations={%region_1.1_spmd, %region_2.2_spmd} | conditional | flops 27769856 | bytes 15556884 | solution.py:65
  20.5 21.8 %add_multiply_fusion.2 = (f32[1,8,64,128]{3,2,0,1:T(8,128)S(1)}, f32[1,8,64,128]{3,2,0,1:T(8,128)S(1)}) fusion(f32[]{:T(128)} %bitcast.15, f32[]{:T(128)} %bitcast.14, f32[]{:T(128)} %bitcast.13, f32[]{:T(128)} %bitcast.12, f32[]{:T(128)} %bitcast.11, f32[]{:T(128)} %bitcast.10, f32[]{:T(128)} %bitcast.9, f32[]{:T(128)} %bitcast.8, f32[]{:T(128)} %bitcast.7, ...), kind=kLoop, calls=%fused_computation.84 | loop fusion | flops 9437184 | bytes 672256 | tf_op jit(solution)/shard_map/while/body/eval_jaxpr/cond/branch_1_fun/mul | solution.py:32
  43.0 11.9 add_multiply_fusion.1
  54.9 11.7 add_multiply_fusion
  66.9 19.7 %add_multiply_fusion.5 = (f32[1,8,64]{2,1,0:T(8,128)S(1)}, f32[1,8,64]{2,1,0:T(8,128)S(1)}) fusion(f32[]{:T(128)} %bitcast.15, f32[]{:T(128)} %bitcast.14, f32[]{:T(128)} %bitcast.13, f32[]{:T(128)} %bitcast.12, f32[]{:T(128)} %bitcast.11, f32[]{:T(128)} %bitcast.10, f32[]{:T(128)} %bitcast.9, f32[]{:T(128)} %bitcast.8, f32[]{:T(128)} %bitcast.7, ...), kind=kLoop, calls=%fused_computation.248 | loop fusion | flops 73728 | bytes 5252 | tf_op jit(solution)/shard_map/while/body/eval_jaxpr/cond/branch_1_fun/mul | solution.py:32
  96.5 10.0 add_multiply_fusion.4
  119.3 91.4 %conditional.2 = (f32[1,4,64,128]{3,2,1,0:T(8,128)S(1)}) conditional(s32[]{:T(128)} %bitcast.339, () %tuple.167, (bf16[16,8,64,128]{3,2,1,0:T(8,128)(2,1)}, s32[]{:T(128)}, f32[3,16]{1,0:T(4,128)S(1)}, f32[16]{0:T(128)S(1)}, bf16[16,8,64]{2,1,0:T(8,128)(2,1)S(1)}) %tuple.168), branch_computations={%region_1.1_spmd, %region_2.2_spmd} | conditional | flops 27769856 | bytes 15556884 | solution.py:65
  121.5 21.8 %add_multiply_fusion.2 = (f32[1,8,64,128]{3,2,0,1:T(8,128)S(1)}, f32[1,8,64,128]{3,2,0,1:T(8,128)S(1)}) fusion(f32[]{:T(128)} %bitcast.15, f32[]{:T(128)} %bitcast.14, f32[]{:T(128)} %bitcast.13, f32[]{:T(128)} %bitcast.12, f32[]{:T(128)} %bitcast.11, f32[]{:T(128)} %bitcast.10, f32[]{:T(128)} %bitcast.9, f32[]{:T(128)} %bitcast.8, f32[]{:T(128)} %bitcast.7, ...), kind=kLoop, calls=%fused_computation.84 | loop fusion | flops 9437184 | bytes 672256 | tf_op jit(solution)/shard_map/while/body/eval_jaxpr/cond/branch_1_fun/mul | solution.py:32
  144.0 11.9 add_multiply_fusion.1
  155.9 11.7 add_multiply_fusion
  167.9 19.7 %add_multiply_fusion.5 = (f32[1,8,64]{2,1,0:T(8,128)S(1)}, f32[1,8,64]{2,1,0:T(8,128)S(1)}) fusion(f32[]{:T(128)} %bitcast.15, f32[]{:T(128)} %bitcast.14, f32[]{:T(128)} %bitcast.13, f32[]{:T(128)} %bitcast.12, f32[]{:T(128)} %bitcast.11, f32[]{:T(128)} %bitcast.10, f32[]{:T(128)} %bitcast.9, f32[]{:T(128)} %bitcast.8, f32[]{:T(128)} %bitcast.7, ...), kind=kLoop, calls=%fused_computation.248 | loop fusion | flops 73728 | bytes 5252 | tf_op jit(solution)/shard_map/while/body/eval_jaxpr/cond/branch_1_fun/mul | solution.py:32
  218.4 91.4 %conditional.2 = (f32[1,4,64,128]{3,2,1,0:T(8,128)S(1)}) conditional(s32[]{:T(128)} %bitcast.339, () %tuple.167, (bf16[16,8,64,128]{3,2,1,0:T(8,128)(2,1)}, s32[]{:T(128)}, f32[3,16]{1,0:T(4,128)S(1)}, f32[16]{0:T(128)S(1)}, bf16[16,8,64]{2,1,0:T(8,128)(2,1)S(1)}) %tuple.168), branch_computations={%region_1.1_spmd, %region_2.2_spmd} | conditional | flops 27769856 | bytes 15556884 | solution.py:65
  220.6 21.8 %add_multiply_fusion.2 = (f32[1,8,64,128]{3,2,0,1:T(8,128)S(1)}, f32[1,8,64,128]{3,2,0,1:T(8,128)S(1)}) fusion(f32[]{:T(128)} %bitcast.15, f32[]{:T(128)} %bitcast.14, f32[]{:T(128)} %bitcast.13, f32[]{:T(128)} %bitcast.12, f32[]{:T(128)} %bitcast.11, f32[]{:T(128)} %bitcast.10, f32[]{:T(128)} %bitcast.9, f32[]{:T(128)} %bitcast.8, f32[]{:T(128)} %bitcast.7, ...), kind=kLoop, calls=%fused_computation.84 | loop fusion | flops 9437184 | bytes 672256 | tf_op jit(solution)/shard_map/while/body/eval_jaxpr/cond/branch_1_fun/mul | solution.py:32
  243.1 11.9 add_multiply_fusion.1
  255.0 11.7 add_multiply_fusion
  267.0 19.7 %add_multiply_fusion.5 = (f32[1,8,64]{2,1,0:T(8,128)S(1)}, f32[1,8,64]{2,1,0:T(8,128)S(1)}) fusion(f32[]{:T(128)} %bitcast.15, f32[]{:T(128)} %bitcast.14, f32[]{:T(128)} %bitcast.13, f32[]{:T(128)} %bitcast.12, f32[]{:T(128)} %bitcast.11, f32[]{:T(128)} %bitcast.10, f32[]{:T(128)} %bitcast.9, f32[]{:T(128)} %bitcast.8, f32[]{:T(128)} %bitcast.7, ...), kind=kLoop, calls=%fused_computation.248 | loop fusion | flops 73728 | bytes 5252 | tf_op jit(solution)/shard_map/while/body/eval_jaxpr/cond/branch_1_fun/mul | solution.py:32
  313.7 91.4 %conditional.2 = (f32[1,4,64,128]{3,2,1,0:T(8,128)S(1)}) conditional(s32[]{:T(128)} %bitcast.339, () %tuple.167, (bf16[16,8,64,128]{3,2,1,0:T(8,128)(2,1)}, s32[]{:T(128)}, f32[3,16]{1,0:T(4,128)S(1)}, f32[16]{0:T(128)S(1)}, bf16[16,8,64]{2,1,0:T(8,128)(2,1)S(1)}) %tuple.168), branch_computations={%region_1.1_spmd, %region_2.2_spmd} | conditional | flops 27769856 | bytes 15556884 | solution.py:65
  315.8 21.8 %add_multiply_fusion.2 = (f32[1,8,64,128]{3,2,0,1:T(8,128)S(1)}, f32[1,8,64,128]{3,2,0,1:T(8,128)S(1)}) fusion(f32[]{:T(128)} %bitcast.15, f32[]{:T(128)} %bitcast.14, f32[]{:T(128)} %bitcast.13, f32[]{:T(128)} %bitcast.12, f32[]{:T(128)} %bitcast.11, f32[]{:T(128)} %bitcast.10, f32[]{:T(128)} %bitcast.9, f32[]{:T(128)} %bitcast.8, f32[]{:T(128)} %bitcast.7, ...), kind=kLoop, calls=%fused_computation.84 | loop fusion | flops 9437184 | bytes 672256 | tf_op jit(solution)/shard_map/while/body/eval_jaxpr/cond/branch_1_fun/mul | solution.py:32
  338.3 11.9 add_multiply_fusion.1
  350.2 11.7 add_multiply_fusion
  362.2 19.7 %add_multiply_fusion.5 = (f32[1,8,64]{2,1,0:T(8,128)S(1)}, f32[1,8,64]{2,1,0:T(8,128)S(1)}) fusion(f32[]{:T(128)} %bitcast.15, f32[]{:T(128)} %bitcast.14, f32[]{:T(128)} %bitcast.13, f32[]{:T(128)} %bitcast.12, f32[]{:T(128)} %bitcast.11, f32[]{:T(128)} %bitcast.10, f32[]{:T(128)} %bitcast.9, f32[]{:T(128)} %bitcast.8, f32[]{:T(128)} %bitcast.7, ...), kind=kLoop, calls=%fused_computation.248 | loop fusion | flops 73728 | bytes 5252 | tf_op jit(solution)/shard_map/while/body/eval_jaxpr/cond/branch_1_fun/mul | solution.py:32
  405.8 35.4 %while.24 = (s32[]{:T(128)}, f32[4,64,144]{2,1,0:T(8,128)S(1)}, f32[16,4,64,128]{3,2,1,0:T(8,128)}, s32[]{:T(128)}, s32[]{:T(128)}, /*index=5*/s32[]{}) while((s32[]{:T(128)}, f32[4,64,144]{2,1,0:T(8,128)S(1)}, f32[16,4,64,128]{3,2,1,0:T(8,128)}, s32[]{:T(128)}, s32[]{:T(128)}, /*index=5*/s32[]{}) %tuple.173), condition=%wide.region_5.6_spmd, body=%wide.region_4.5_spmd.sunk | while | flops 73731 | bytes 753761 | solution.py:79
  471.9 35.1 %collective-permute-done.1 = f32[4,256,768]{2,0,1:T(4,128)} collective-permute-done((f32[4,256,768]{2,0,1:T(4,128)}, f32[4,256,768]{2,0,1:T(4,128)}, u32[]{:S(2)}, u32[]{:S(2)}) %collective-permute-start.1) | collective-permute-done | bytes 3145760 | tf_op jit(solution)/shard_map/ppermute | solution.py:19
  514.7 188.7 %collective-permute-start.2 = (f32[4,128,768]{2,0,1:T(4,128)}, f32[4,128,768]{2,0,1:T(4,128)S(1)}, u32[]{:S(2)}, u32[]{:S(2)}) collective-permute-start(f32[4,128,768]{2,0,1:T(4,128)} %get-tuple-element.396), channel_id=1, source_target_pairs={{0,2},{1,3},{2,0},{3,1},{4,6},{5,7},{6,4},{7,5},{8,10},{9,11},{10,... | collective-permute-start | bytes 4718600 | tf_op jit(solution)/shard_map/ppermute | solution.py:19
  703.9 34.3 %collective-permute-done.2 = f32[4,128,768]{2,0,1:T(4,128)S(1)} collective-permute-done((f32[4,128,768]{2,0,1:T(4,128)}, f32[4,128,768]{2,0,1:T(4,128)S(1)}, u32[]{:S(2)}, u32[]{:S(2)}) %collective-permute-start.2) | collective-permute-done | bytes 1572896 | tf_op jit(solution)/shard_map/ppermute | solution.py:19
  739.7 99.8 %collective-permute-start.3 = (f32[4,64,768]{2,0,1:T(4,128)S(1)}, f32[4,64,768]{2,0,1:T(4,128)S(1)}, u32[]{:S(2)}, u32[]{:S(2)}) collective-permute-start(f32[4,64,768]{2,0,1:T(4,128)S(1)} %get-tuple-element.398), channel_id=1, source_target_pairs={{0,4},{1,5},{2,6},{3,7},{4,0},{5,1},{6,2},{7,3},{8,12},{9,13},{10,... | collective-permute-start | bytes 2359304 | tf_op jit(solution)/shard_map/ppermute | solution.py:19
  839.8 33.7 %collective-permute-done.3 = f32[4,64,768]{2,0,1:T(4,128)S(1)} collective-permute-done((f32[4,64,768]{2,0,1:T(4,128)S(1)}, f32[4,64,768]{2,0,1:T(4,128)S(1)}, u32[]{:S(2)}, u32[]{:S(2)}) %collective-permute-start.3) | collective-permute-done | bytes 786464 | tf_op jit(solution)/shard_map/ppermute | solution.py:19
  874.4 381.6 %collective-permute-start.4 = (f32[4,32,768]{2,0,1:T(4,128)S(1)}, f32[4,32,768]{2,0,1:T(4,128)S(1)}, u32[]{:S(2)}, u32[]{:S(2)}) collective-permute-start(f32[4,32,768]{2,0,1:T(4,128)S(1)} %get-tuple-element.400), channel_id=1, source_target_pairs={{0,8},{1,9},{2,10},{3,11},{4,12},{5,13},{6,14},{7,15},{8,0},{9,1},... | collective-permute-start | bytes 1179656 | tf_op jit(solution)/shard_map/ppermute | solution.py:19
  1266.0 121.5 %collective-permute-start.5 = (f32[4,16,768]{2,0,1:T(4,128)S(1)}, f32[4,16,768]{2,0,1:T(4,128)S(1)}, u32[]{:S(2)}, u32[]{:S(2)}) collective-permute-start(f32[4,16,768]{2,0,1:T(4,128)S(1)} %get-tuple-element.402), channel_id=1, source_target_pairs={{0,16},{16,0},{32,48},{48,32},{64,80},{80,64},{96,112},{112,96},{1... | collective-permute-start | bytes 589832 | tf_op jit(solution)/shard_map/ppermute | solution.py:19
  1388.8 156.3 %collective-permute-start.6 = (f32[4,8,768]{2,0,1:T(4,128)S(1)}, f32[4,8,768]{2,0,1:T(4,128)S(1)}, u32[]{:S(2)}, u32[]{:S(2)}) collective-permute-start(f32[4,8,768]{2,0,1:T(4,128)S(1)} %get-tuple-element.404), channel_id=1, source_target_pairs={{0,32},{16,48},{32,0},{48,16},{64,96},{80,112},{96,64},{112,80},{1... | collective-permute-start | bytes 294920 | tf_op jit(solution)/shard_map/ppermute | solution.py:19
  1548.2 197.4 %collective-permute-start.7 = (f32[4,4,768]{2,0,1:T(4,128)S(1)}, f32[4,4,768]{2,0,1:T(4,128)S(1)}, u32[]{:S(2)}, u32[]{:S(2)}) collective-permute-start(f32[4,4,768]{2,0,1:T(4,128)S(1)} %get-tuple-element.406), channel_id=1, source_target_pairs={{0,64},{16,80},{32,96},{48,112},{64,0},{80,16},{96,32},{112,48},{1... | collective-permute-start | bytes 147464 | tf_op jit(solution)/shard_map/ppermute | solution.py:19
  (359 shorter events, 227.2 us)
Async XLA Ops:
  2.3 7.1 copy-start
  2.3 7.1 copy-start.1
  2.3 7.1 copy-start.2
  4.5 4.8 collective-permute-start
  468.8 38.3 %collective-permute-start.1 = (f32[4,256,768]{2,0,1:T(4,128)}, f32[4,256,768]{2,0,1:T(4,128)}, u32[]{:S(2)}, u32[]{:S(2)}) collective-permute-start(f32[4,256,768]{2,0,1:T(4,128)} %get-tuple-element.394), channel_id=1, source_target_pairs={{0,1},{1,0},{2,3},{3,2},{4,5},{5,4},{6,7},{7,6},{8,9},{9,8},{10,11... | collective-permute-start | bytes 9437192 | tf_op jit(solution)/shard_map/ppermute | solution.py:19
  514.7 223.5 %collective-permute-start.2 = (f32[4,128,768]{2,0,1:T(4,128)}, f32[4,128,768]{2,0,1:T(4,128)S(1)}, u32[]{:S(2)}, u32[]{:S(2)}) collective-permute-start(f32[4,128,768]{2,0,1:T(4,128)} %get-tuple-element.396), channel_id=1, source_target_pairs={{0,2},{1,3},{2,0},{3,1},{4,6},{5,7},{6,4},{7,5},{8,10},{9,11},{10,... | collective-permute-start | bytes 4718600 | tf_op jit(solution)/shard_map/ppermute | solution.py:19
  739.7 133.8 %collective-permute-start.3 = (f32[4,64,768]{2,0,1:T(4,128)S(1)}, f32[4,64,768]{2,0,1:T(4,128)S(1)}, u32[]{:S(2)}, u32[]{:S(2)}) collective-permute-start(f32[4,64,768]{2,0,1:T(4,128)S(1)} %get-tuple-element.398), channel_id=1, source_target_pairs={{0,4},{1,5},{2,6},{3,7},{4,0},{5,1},{6,2},{7,3},{8,12},{9,13},{10,... | collective-permute-start | bytes 2359304 | tf_op jit(solution)/shard_map/ppermute | solution.py:19
  874.4 391.2 %collective-permute-start.4 = (f32[4,32,768]{2,0,1:T(4,128)S(1)}, f32[4,32,768]{2,0,1:T(4,128)S(1)}, u32[]{:S(2)}, u32[]{:S(2)}) collective-permute-start(f32[4,32,768]{2,0,1:T(4,128)S(1)} %get-tuple-element.400), channel_id=1, source_target_pairs={{0,8},{1,9},{2,10},{3,11},{4,12},{5,13},{6,14},{7,15},{8,0},{9,1},... | collective-permute-start | bytes 1179656 | tf_op jit(solution)/shard_map/ppermute | solution.py:19
  1266.0 122.6 %collective-permute-start.5 = (f32[4,16,768]{2,0,1:T(4,128)S(1)}, f32[4,16,768]{2,0,1:T(4,128)S(1)}, u32[]{:S(2)}, u32[]{:S(2)}) collective-permute-start(f32[4,16,768]{2,0,1:T(4,128)S(1)} %get-tuple-element.402), channel_id=1, source_target_pairs={{0,16},{16,0},{32,48},{48,32},{64,80},{80,64},{96,112},{112,96},{1... | collective-permute-start | bytes 589832 | tf_op jit(solution)/shard_map/ppermute | solution.py:19
  1388.8 159.3 %collective-permute-start.6 = (f32[4,8,768]{2,0,1:T(4,128)S(1)}, f32[4,8,768]{2,0,1:T(4,128)S(1)}, u32[]{:S(2)}, u32[]{:S(2)}) collective-permute-start(f32[4,8,768]{2,0,1:T(4,128)S(1)} %get-tuple-element.404), channel_id=1, source_target_pairs={{0,32},{16,48},{32,0},{48,16},{64,96},{80,112},{96,64},{112,80},{1... | collective-permute-start | bytes 294920 | tf_op jit(solution)/shard_map/ppermute | solution.py:19
  1548.2 198.9 %collective-permute-start.7 = (f32[4,4,768]{2,0,1:T(4,128)S(1)}, f32[4,4,768]{2,0,1:T(4,128)S(1)}, u32[]{:S(2)}, u32[]{:S(2)}) collective-permute-start(f32[4,4,768]{2,0,1:T(4,128)S(1)} %get-tuple-element.406), channel_id=1, source_target_pairs={{0,64},{16,80},{32,96},{48,112},{64,0},{80,16},{96,32},{112,48},{1... | collective-permute-start | bytes 147464 | tf_op jit(solution)/shard_map/ppermute | solution.py:19
  1747.2 4.6 collective-permute-start.8
  1751.8 5.9 collective-permute-start.9
where the time goes:
time: 1780 us; the launch traced here: 1760 us
  starting transfers between devices  1160 us (65%)
  other arithmetic  381 us (21%)
  waiting for transfers between devices  125 us (7%)
  local copies, waits for them, and re-layouts  84.5 us (5%)
    ppermute x9, starting transfers between devices, partner(): lax.ppermute(value, axis, [(i, i ^ 1 << bit) for i in range(lax.axis_size...  1150 us
    mul x8, other arithmetic, classify(): shades[0] * opacity  166 us
    ppermute x9, waiting for transfers between devices, partner(): lax.ppermute(value, axis, [(i, i ^ 1 << bit) for i in range(lax.axis_size...  125 us
    mul x8, other arithmetic, classify(): shades[1] * opacity  87.6 us
    mul x8, other arithmetic, classify(): shades[2] * opacity  86.5 us
  transfers between devices with their start and end apart: 10, of which 10 were waited for; matrix products, arithmetic and copies ran while one was open for 0% of the time, Pallas kernels for 0%

commit v1 on v0

v1 whole, which is shorter than its diff:
```python
import functools

import jax
import jax.numpy as jnp
from jax import lax
from jax.experimental import pallas as pl
from jax.experimental.pallas import tpu as pltpu
from jax.sharding import PartitionSpec as P

BZ = 8
LIMIT = 3.0
KNOTS = 16
LANES = 128
GROUP = 16
STEPS = 4
F32 = jnp.float32


def lane_ids(rows):
    return lax.broadcasted_iota(jnp.int32, (rows, LANES), 1)


def pick(table, index):
    return jnp.take_along_axis(table, index, axis=1, mode="promise_in_bounds")


def build_tables(color_ref, opacity_ref, pad_ref, table_ref):
    pad_ref[...] = jnp.zeros_like(pad_ref)
    pad_ref[0:3, 0:KNOTS] = color_ref[...]
    pad_ref[3:4, 0:KNOTS] = opacity_ref[...]
    upper = pad_ref[...]
    lower = pltpu.roll(upper, 1, 1)
    slope = upper - lower
    base = lower - slope * lane_ids(8).astype(F32)
    for n in range(4):
        table_ref[n] = jnp.broadcast_to(base[n:n + 1], (GROUP, LANES))
        table_ref[4 + n] = jnp.broadcast_to(slope[n:n + 1], (GROUP, LANES))


def classify(values, tables):
    scale = (KNOTS - 1) / (2.0 * LIMIT)
    place = jnp.clip(values * scale + (LIMIT * scale + 1.0), 0.0, KNOTS + 1.0)
    index = place.astype(jnp.int32)
    return [pick(tables[n], index) + pick(tables[4 + n], index) * place for n in range(4)]


def render_kernel(flag_ref, color_ref, opacity_ref, volume_ref, front_ref, tail_ref,
                  pad_ref, table_ref, run_ref, done_ref):
    step = pl.program_id(0)
    rows_all = front_ref.shape[1]
    groups = rows_all // GROUP
    bricks = volume_ref.shape[0] // BZ

    @pl.when(step == 0)
    def _():
        build_tables(color_ref, opacity_ref, pad_ref, table_ref)
        for ref in (run_ref, done_ref):
            ref[0:3] = jnp.zeros((3, rows_all, LANES), F32)
            ref[3] = jnp.ones((rows_all, LANES), F32)

    lane = lane_ids(GROUP)

    def one(item, carry):
        local = item // groups
        brick = step * bricks + local
        rows = pl.ds(pl.multiple_of(item % groups * GROUP, GROUP), GROUP)
        tables = [table_ref[n] for n in range(8)]
        for k in range(BZ):
            f = k / BZ
            *shades, alpha = classify(volume_ref[local * BZ + k, rows, :].astype(F32), tables)
            if k == 0:
                here = [alpha * shade for shade in shades]
                clear = 1.0 - alpha
                continue
            moved = alpha * f
            kept = alpha - moved
            weight = clear * kept
            beside = pltpu.roll(clear, LANES - 1, 1) * moved
            here = [h + weight * shade for h, shade in zip(here, shades)]
            if k == 1:
                right = [beside * shade for shade in shades]
            else:
                right = [r + beside * shade for r, shade in zip(right, shades)]
            clear = clear - clear * (kept + pltpu.roll(moved, 1, 1))
        shown = jnp.where(lane == 0, 0.0, flag_ref[brick, 0, 0].astype(F32))
        image = [(h + pltpu.roll(r, 1, 1)) * shown for h, r in zip(here, right)]
        image.append((1.0 - clear) * shown)
        image = [pltpu.roll(value, brick, 1) for value in image]
        leaving = lane == brick - 1
        through = run_ref[3, rows, :]
        done_ref[3, rows, :] = jnp.where(leaving, through, done_ref[3, rows, :])
        through = jnp.where(leaving, 1.0, through)
        for n in range(3):
            sum_n = run_ref[n, rows, :]
            done_ref[n, rows, :] = jnp.where(leaving, sum_n, done_ref[n, rows, :])
            run_ref[n, rows, :] = jnp.where(leaving, 0.0, sum_n) + through * image[n]
        run_ref[3, rows, :] = through - through * image[3]
        return carry

    lax.fori_loop(0, bricks * groups, one, 0)

    @pl.when(step == pl.num_programs(0) - 1)
    def _():
        wide = lane_ids(rows_all)
        total = pl.num_programs(0) * bricks
        for n in range(4):
            last = run_ref[n] if n < 3 else 1.0 - run_ref[n]
            first = done_ref[n] if n < 3 else 1.0 - done_ref[n]
            front_ref[n] = jnp.where(wide < total - 1, first, last)
            tail_ref[n] = jnp.where(wide < total - 1, last, 0.0)


def render(active, tf_color, tf_opacity, volume):
    layers, rows, cols = volume.shape
    out = jax.ShapeDtypeStruct((4, rows, LANES), F32)
    whole = pl.BlockSpec((4, rows, LANES), lambda i: (0, 0, 0))
    return pl.pallas_call(
        render_kernel,
        grid=(STEPS,),
        in_specs=[
            pl.BlockSpec(memory_space=pltpu.SMEM),
            pl.BlockSpec(tf_color.shape, lambda i: (0, 0)),
            pl.BlockSpec(tf_opacity.shape, lambda i: (0, 0)),
            pl.BlockSpec((layers // STEPS, rows, cols), lambda i: (i, 0, 0)),
        ],
        out_specs=[whole, whole],
        out_shape=[out, out],
        scratch_shapes=[
            pltpu.VMEM((8, LANES), F32),
            pltpu.VMEM((8, GROUP, LANES), F32),
            pltpu.VMEM((4, rows, LANES), F32),
            pltpu.VMEM((4, rows, LANES), F32),
        ],
        cost_estimate=pl.CostEstimate(flops=40_000_000, bytes_accessed=2_400_000, transcendentals=0),
        compiler_params=pltpu.CompilerParams(vmem_limit_bytes=32 * 1024 * 1024),
        name="render",
    )(active, tf_color, tf_opacity, volume)


def deal_kernel(flag_ref, color_ref, opacity_ref, column_ref, rim_ref, front_ref, tail_ref, out_ref,
                pad_ref, table_ref, column_f32, rim_f32):
    build_tables(color_ref, opacity_ref, pad_ref, table_ref)
    tables = [table_ref[n] for n in range(8)]
    out_ref[...] = jnp.zeros_like(out_ref)
    total, rows = column_ref.shape
    bricks = total // BZ
    half = rows // 2
    column_f32[:, 0:rows] = column_ref[...].astype(F32)
    rim_f32[:, 0:rows] = rim_ref[...].astype(F32)
    start = lax.axis_index("gx") * LANES + lax.axis_index("gz") * bricks
    targets = out_ref.shape[0]
    lane = lane_ids(GROUP)
    flags = jnp.broadcast_to(flag_ref[...].astype(F32), (bricks, LANES))
    to_alpha = lane % half + 3 * half
    for parity in range(2):
        spread = lane % half * 2 + parity

        def shaded(ref, k):
            values = pick(ref[pl.ds(k, bricks, stride=BZ), :], spread)
            red, green, blue, alpha = classify(values, tables)
            shade = jnp.where(lane < half, red, jnp.where(lane < 2 * half, green, blue))
            return alpha * jnp.where(lane < 3 * half, shade, 1.0), alpha

        image = jnp.zeros((bricks, LANES), F32)
        clear = jnp.ones((bricks, LANES), F32)
        for k in range(BZ):
            f = k / BZ
            sample, alpha = shaded(column_f32, k)
            if k:
                beside, beside_alpha = shaded(rim_f32, k)
                sample = (1.0 - f) * sample + f * beside
                alpha = (1.0 - f) * alpha + f * beside_alpha
            image = image + clear * sample
            clear = clear - clear * alpha
        image = image * flags
        near = jnp.concatenate([front_ref[n, pl.ds(parity, half, stride=2), :] for n in range(4)], axis=0).T
        far = jnp.concatenate([tail_ref[n, pl.ds(parity, half, stride=2), :] for n in range(4)], axis=0).T
        for m in range(LANES // GROUP + 1):
            place = lax.rem(start + parity * (targets // 2) + m * GROUP, targets)
            piece = near[m * GROUP:(m + 1) * GROUP] if m < LANES // GROUP else far[:GROUP]
            if m == 0:
                piece = piece + (1.0 - pick(piece, to_alpha)) * image
            out_ref[pl.ds(pl.multiple_of(place, GROUP), GROUP), :] = piece


def deal(active, tf_color, tf_opacity, column, rim, front, tail, targets):
    return pl.pallas_call(
        deal_kernel,
        out_shape=jax.ShapeDtypeStruct((targets, LANES), F32),
        scratch_shapes=[
            pltpu.VMEM((8, LANES), F32),
            pltpu.VMEM((8, GROUP, LANES), F32),
            pltpu.VMEM((column.shape[0], LANES), F32),
            pltpu.VMEM((column.shape[0], LANES), F32),
        ],
        compiler_params=pltpu.CompilerParams(vmem_limit_bytes=32 * 1024 * 1024),
        name="deal",
    )(active, tf_color, tf_opacity, column, rim, front, tail)


def gather_kernel(across, down, depth, bricks, arrived_ref, out_ref):
    targets = across * down * depth
    me = (lax.axis_index("gx") * down + lax.axis_index("gy")) * depth + lax.axis_index("gz")
    half = LANES // 4
    lane = lane_ids(down)
    to_alpha = lane % half + 3 * half
    total = [jnp.zeros((down, LANES), F32) for k in range(3)]
    clear = [jnp.ones((down, LANES), F32) for k in range(3)]
    for front in range(depth):
        for x in reversed(range(across)):
            start = x * LANES + front * bricks
            behind = lax.rem(me - start + 2 * targets, targets)
            slot = jnp.where(me < start, 1, 0) + jnp.where(behind >= targets // 2, 1, 0)
            piece = arrived_ref[pl.ds(x * down * depth + front, down, stride=depth), :]
            alpha = pick(piece, to_alpha)
            for k in range(3):
                mine = jnp.where(slot == k, 1.0, 0.0)
                total[k] = total[k] + clear[k] * (piece * mine)
                clear[k] = clear[k] - clear[k] * (alpha * mine)
    width = 3 * half
    third = lane % 3
    for c in range(4):
        source = jnp.minimum(lane // 3, half - 1) + c * half
        spread = [pick(value, source) for value in total]
        row = jnp.where(third == 0, spread[0], jnp.where(third == 1, spread[1], spread[2]))
        for y in range(down):
            out_ref[c, 0:1, y * width:(y + 1) * width] = row[y:y + 1, 0:width]


def gather(arrived, across, down, depth, bricks):
    pixels = down * 3 * LANES // 4
    return pl.pallas_call(
        functools.partial(gather_kernel, across, down, depth, bricks),
        out_shape=jax.ShapeDtypeStruct((4, 1, pixels), F32),
        compiler_params=pltpu.CompilerParams(vmem_limit_bytes=32 * 1024 * 1024),
        name="gather",
    )(arrived)


def body(volume, tf_color, tf_opacity, active):
    layers = volume.shape[0]
    bricks = layers // BZ
    across, down, depth = (lax.axis_size(name) for name in ("gx", "gy", "gz"))
    targets = across * down * depth
    opacity = tf_opacity.reshape(1, -1)
    rim = lax.ppermute(volume[:, :, -1], "gx", [(i, i + 1) for i in range(across - 1)])
    column = volume[:, :, 0]
    front, tail = render(active, tf_color, opacity, volume)
    rows = deal(active.reshape(bricks, 1), tf_color, opacity, column, rim, front, tail, targets)
    arrived = lax.all_to_all(rows, ("gx", "gy", "gz"), 0, 0, tiled=True)
    return gather(arrived, across, down, depth, bricks)


def solution(mesh):
    placed = (P("gz", "gy", "gx"), P(), P(), P("gz", "gy", "gx"))
    return jax.shard_map(
        body,
        mesh=mesh,
        in_specs=placed,
        out_specs=P(None, ("gx", "gy", "gz"), None),
        check_vma=False,
    )
```

time: 1780 us -> 107 us (0.06); the launches traced: 1760 us -> 107 us
  starting transfers between devices: 1160 us -> 3.94 us
  other arithmetic: 381 us -> 0 us
  waiting for transfers between devices: 125 us -> 0.01 us
  local copies, waits for them, and re-layouts: 84.5 us -> 9.58 us
  blocking collectives: 0 us -> 48 us
  Pallas kernels: 0 us -> 45.2 us
    ppermute x10 -> x1, starting transfers between devices: 1160 us -> 3.94 us  [body(): lax.ppermute(volume[:, :, -1], 'gx', [(i, i + 1) for i in range(across -...]
    mul x68 -> x0, other arithmetic: 342 us -> none  [the longest x8 166 us: classify(): shades[0] * opacity]
    ppermute x10 -> x1, waiting for transfers between devices: 125 us -> 0.01 us  [body(): lax.ppermute(volume[:, :, -1], 'gx', [(i, i + 1) for i in range(across -...]
    all_to_all x0 -> x1, blocking collectives: none -> 48 us  [body(): arrived = lax.all_to_all(rows, ('gx', 'gy', 'gz'), 0, 0, tiled=True)]
    pallas_call x0 -> x3, Pallas kernels: none -> 45.2 us  [the longest x1 40.7 us: render(): pl.pallas_call(render_kernel, grid=(STEPS,), in_specs=[pl.BlockSpec(memor...]
    dynamic_update_slice x33 -> x0, local copies, waits for them, and re-layouts: 31.5 us -> none  [the longest x16 17.4 us: place_brick(): return lax.dynamic_update_slice_in_dim(window, merged, brick_index, 2)]
    add x44 -> x0, other arithmetic: 20.3 us -> none  [the longest x40 19.8 us: composite(): return nearer + (1.0 - nearer[3:4]) * farther]
  transfers between devices with their start and end apart: 10 -> 1, of which waited for: 10 -> 0; matrix products, arithmetic and copies ran while one was open for 0% -> 2% of each run, Pallas kernels for 0% -> 38%
where the time goes in v1:
time: 107 us
  blocking collectives  48 us (45%)
  Pallas kernels  45.2 us (42%)
  local copies, waits for them, and re-layouts  9.58 us (9%)
  starting transfers between devices  3.94 us (4%)
    all_to_all x1, blocking collectives, body(): arrived = lax.all_to_all(rows, ('gx', 'gy', 'gz'), 0, 0, tiled=True)  48 us
    pallas_call x1, Pallas kernels, render(): pl.pallas_call(render_kernel, grid=(STEPS,), in_specs=[pl.BlockSpec(memor...  40.7 us
    slice x1, local copies, waits for them, and re-layouts, body(): volume[:, :, -1]  4.98 us
    unnamed x11, local copies, waits for them, and re-layouts  4.52 us
    ppermute x1, starting transfers between devices, body(): lax.ppermute(volume[:, :, -1], 'gx', [(i, i + 1) for i in range(across -...  3.94 us
    pallas_call x1, Pallas kernels, deal(): pl.pallas_call(deal_kernel, out_shape=jax.ShapeDtypeStruct((targets, LANE...  3.35 us
  transfers between devices with their start and end apart: 1, of which 0 were waited for; matrix products, arithmetic and copies ran while one was open for 2% of the time, Pallas kernels for 38%

profile of v1, /device:TPU:1, one launch (start us, length us, event | category | flops | bytes accessed | tf_op | source)
XLA Modules:
  0.0 106.8 jit_solution(13114283852723649491)
XLA Ops:
  0.0 5.0 %fusion = (bf16[128,64,1]{2,1,0:T(8,128)(2,1)}, bf16[128,64,1]{2,1,0:T(8,128)(2,1)}) fusion(bf16[128,64,128]{2,1,0:T(8,128)(2,1)} %volume_ref.1), kind=kLoop, calls=%fused_computation | loop fusion | bytes 65536 | tf_op jit(solution)/shard_map/slice | solution.py:246
  5.0 0.0 copy-start.3
  5.0 0.0 copy-start
  5.0 0.0 copy-start.1
  5.0 0.0 copy-start.2
  5.0 2.3 %copy.15 = bf16[128,64,1]{1,0,2:T(8,128)(2,1)S(1)} copy(bf16[128,64,1]{2,1,0:T(8,128)(2,1)} %get-tuple-element.9) | data formatting | bytes 32768
  7.3 3.9 %collective-permute-start = (bf16[128,64]{1,0:T(8,128)(2,1)S(1)}, bf16[128,64]{1,0:T(8,128)(2,1)S(1)}, u32[]{:S(2)}, u32[]{:S(2)}) collective-permute-start(bf16[128,64]{1,0:T(8,128)(2,1)S(1)} %bitcast.13), channel_id=1, source_target_pairs={{0,128},{128,256},{256,384},{1,129},{129,257},{257,385},{2,130},{1... | collective-permute-start | bytes 49160 | tf_op jit(solution)/shard_map/ppermute | solution.py:246
  11.2 0.0 copy-done.3
  11.2 0.1 copy.11.flag_ref
  11.3 0.1 copy.12.flag_ref
  11.4 2.1 %copy.14 = bf16[128,64,1]{1,0,2:T(8,128)(2,1)S(1)} copy(bf16[128,64,1]{2,1,0:T(8,128)(2,1)} %get-tuple-element.10) | data formatting | bytes 32768
  13.5 0.0 copy-done
  13.6 0.0 copy-done.1
  13.6 0.0 copy-done.2
  13.6 40.7 %render.1 = (f32[4,64,128]{2,1,0:T(8,128)S(1)}, f32[4,64,128]{2,1,0:T(8,128)S(1)}) custom-call(s32[16,1,1]{2,1,0:T(1,128)S(1)} %copy.11.flag_ref, f32[3,16]{1,0:T(4,128)S(1)} %copy-done.1, f32[1,16]{1,0:T(1,128)S(1)} %bitcast.11, bf16[128,64,128]{2,1,0:T(8,128)(2,1)S(1)} %copy-done), custom_call_target="tpu_custom_call" | custom-call | flops 40000000 | bytes 2400000 | tf_op jit(solution)/shard_map/render/pallas_call | solution.py:117
  54.3 0.0 collective-permute-done.rim_ref
  54.3 3.4 %deal.1 = f32[512,128]{1,0:T(8,128)S(1)} custom-call(s32[16,1]{1,0:T(8,128)S(1)} %copy.12.flag_ref, f32[3,16]{1,0:T(4,128)S(1)} %copy-done.1, f32[1,16]{1,0:T(1,128)S(1)} %bitcast.12, bf16[128,64]{1,0:T(8,128)(2,1)S(1)} %bitcast.10, bf16[128,64]{1,0:T(8,128)(2,1)S(1)} %collective-permute-done.rim_ref, f32[4,64,128]{2,1,0:T(8,128)S(1)} %get-tuple-element.7.front_ref, ...), custom_call_target="tpu_custom_call" | custom-call | tf_op jit(solution)/shard_map/deal/pallas_call | solution.py:187
  57.6 48.0 %all_to_all.11 = f32[512,1,128]{2,1,0:T(1,128)S(1)} all-to-all(f32[512,1,128]{2,1,0:T(1,128)S(1)} %bitcast.8), channel_id=1, replica_groups=mesh['gx'=4,'gy'=8,'gz'=16] {'gx','gy','gz'}, dimensions={0} | all-to-all | bytes 524288 | tf_op jit(solution)/shard_map/all_to_all | solution.py:250
  105.6 1.1 %gather.1 = f32[4,1,768]{2,1,0:T(1,128)} custom-call(f32[512,128]{1,0:T(8,128)S(1)} %bitcast.9), custom_call_target="tpu_custom_call" | custom-call | tf_op jit(solution)/shard_map/gather/pallas_call | solution.py:232
Async XLA Ops:
  5.0 6.3 %copy-start.3 = (s32[16,1,1]{0,2,1:T(1,128)S(1)}, s32[16,1,1]{0,2,1:T(1,128)}, u32[]{:S(2)}) copy-start(s32[16,1,1]{0,2,1:T(1,128)} %param.7) | copy-start | bytes 196
  5.0 8.6 %copy-start = (bf16[128,64,128]{2,1,0:T(8,128)(2,1)S(1)}, bf16[128,64,128]{2,1,0:T(8,128)(2,1)}, u32[]{:S(2)}) copy-start(bf16[128,64,128]{2,1,0:T(8,128)(2,1)} %volume_ref.1) | copy-start | bytes 6291460
  5.0 8.6 %copy-start.1 = (f32[3,16]{1,0:T(4,128)S(1)}, f32[3,16]{1,0:T(4,128)}, u32[]{:S(2)}) copy-start(f32[3,16]{1,0:T(4,128)} %color_ref.3) | copy-start | bytes 580
  5.0 8.6 %copy-start.2 = (f32[16]{0:T(128)S(1)}, f32[16]{0:T(128)}, u32[]{:S(2)}) copy-start(f32[16]{0:T(128)} %param.6) | copy-start | bytes 196
  7.3 47.0 %collective-permute-start = (bf16[128,64]{1,0:T(8,128)(2,1)S(1)}, bf16[128,64]{1,0:T(8,128)(2,1)S(1)}, u32[]{:S(2)}, u32[]{:S(2)}) collective-permute-start(bf16[128,64]{1,0:T(8,128)(2,1)S(1)} %bitcast.13), channel_id=1, source_target_pairs={{0,128},{128,256},{256,384},{1,129},{129,257},{257,385},{2,130},{1... | collective-permute-start | bytes 49160 | tf_op jit(solution)/shard_map/ppermute | solution.py:246

commit v2 on v1

--- a/solution.py
+++ b/solution.py
@@ -13,6 +13,8 @@
 LANES = 128
 GROUP = 16
 STEPS = 4
+UNROLL = 4
+CHAINED = (2, 5)
 F32 = jnp.float32
 
 
@@ -41,11 +43,26 @@
     scale = (KNOTS - 1) / (2.0 * LIMIT)
     place = jnp.clip(values * scale + (LIMIT * scale + 1.0), 0.0, KNOTS + 1.0)
     index = place.astype(jnp.int32)
-    return [pick(tables[n], index) + pick(tables[4 + n], index) * place for n in range(4)]
+    got = [pick(table, index) for table in tables]
+    return [got[n] + got[4 + n] * place for n in range(4)]
+
+
+def climb(values, knot_ref):
+    scale = (KNOTS - 1) / (2.0 * LIMIT)
+    place = values * scale + (LIMIT * scale + 1.0)
+    base = [jnp.zeros_like(values) for n in range(4)]
+    slope = [knot_ref[4 + n, 0] for n in range(4)]
+    for k in range(KNOTS + 2):
+        above = place >= float(k)
+        for n in range(4):
+            if k:
+                base[n] = jnp.where(above, knot_ref[n, k], base[n])
+            slope[n] = jnp.where(above, knot_ref[4 + n, k], slope[n] if k else 0.0)
+    return [base[n] + slope[n] * place for n in range(4)]
 
 
 def render_kernel(flag_ref, color_ref, opacity_ref, volume_ref, front_ref, tail_ref,
-                  pad_ref, table_ref, run_ref, done_ref):
+                  pad_ref, table_ref, run_ref, done_ref, seen_ref, knot_ref):
     step = pl.program_id(0)
     rows_all = front_ref.shape[1]
     groups = rows_all // GROUP
@@ -54,50 +71,71 @@
     @pl.when(step == 0)
     def _():
         build_tables(color_ref, opacity_ref, pad_ref, table_ref)
+        for n in range(8):
+            for k in range(KNOTS + 2):
+                knot_ref[n, k] = pick(table_ref[n, 0:8], jnp.full((8, LANES), k, jnp.int32))
         for ref in (run_ref, done_ref):
             ref[0:3] = jnp.zeros((3, rows_all, LANES), F32)
             ref[3] = jnp.ones((rows_all, LANES), F32)
 
     lane = lane_ids(GROUP)
-
-    def one(item, carry):
-        local = item // groups
+    layers = volume_ref.shape[0]
+
+    def look(layer, carry):
+        tables = [table_ref[n, 0:8] for n in range(8)]
+        for start in range(0, rows_all, GROUP):
+            pair = volume_ref[layer, start:start + GROUP, :].astype(F32)
+            for q in range(0, GROUP, 8):
+                at = start + q
+                if at // 8 in CHAINED:
+                    found = climb(pair[q:q + 8], knot_ref)
+                else:
+                    found = classify(pair[q:q + 8], tables)
+                for n in range(4):
+                    seen_ref[n, layer, at:at + 8, :] = found[n]
+        return carry
+
+    lax.fori_loop(0, layers, look, 0, unroll=UNROLL)
+
+    def one(local, carry):
         brick = step * bricks + local
-        rows = pl.ds(pl.multiple_of(item % groups * GROUP, GROUP), GROUP)
-        tables = [table_ref[n] for n in range(8)]
-        for k in range(BZ):
-            f = k / BZ
-            *shades, alpha = classify(volume_ref[local * BZ + k, rows, :].astype(F32), tables)
-            if k == 0:
-                here = [alpha * shade for shade in shades]
-                clear = 1.0 - alpha
-                continue
-            moved = alpha * f
-            kept = alpha - moved
-            weight = clear * kept
-            beside = pltpu.roll(clear, LANES - 1, 1) * moved
-            here = [h + weight * shade for h, shade in zip(here, shades)]
-            if k == 1:
-                right = [beside * shade for shade in shades]
-            else:
-                right = [r + beside * shade for r, shade in zip(right, shades)]
-            clear = clear - clear * (kept + pltpu.roll(moved, 1, 1))
-        shown = jnp.where(lane == 0, 0.0, flag_ref[brick, 0, 0].astype(F32))
-        image = [(h + pltpu.roll(r, 1, 1)) * shown for h, r in zip(here, right)]
-        image.append((1.0 - clear) * shown)
-        image = [pltpu.roll(value, brick, 1) for value in image]
-        leaving = lane == brick - 1
-        through = run_ref[3, rows, :]
-        done_ref[3, rows, :] = jnp.where(leaving, through, done_ref[3, rows, :])
-        through = jnp.where(leaving, 1.0, through)
-        for n in range(3):
-            sum_n = run_ref[n, rows, :]
-            done_ref[n, rows, :] = jnp.where(leaving, sum_n, done_ref[n, rows, :])
-            run_ref[n, rows, :] = jnp.where(leaving, 0.0, sum_n) + through * image[n]
-        run_ref[3, rows, :] = through - through * image[3]
+        for group in range(groups):
+            rows = slice(group * GROUP, (group + 1) * GROUP)
+            for k in range(BZ):
+                f = k / BZ
+                *shades, alpha = [seen_ref[n, local * BZ + k, rows, :] for n in range(4)]
+                if k == 0:
+                    here = [alpha * shade for shade in shades]
+                    clear = 1.0 - alpha
+                    continue
+                moved = alpha * f
+                kept = alpha - moved
+                weight = clear * kept
+                beside = pltpu.roll(clear, LANES - 1, 1) * moved
+                here = [h + weight * shade for h, shade in zip(here, shades)]
+                if k == 1:
+                    right = [beside * shade for shade in shades]
+                else:
+                    right = [r + beside * shade for r, shade in zip(right, shades)]
+                clear = clear - clear * (kept + pltpu.roll(moved, 1, 1))
+            flag = flag_ref[brick].astype(F32)
+            shown = jnp.where(lane == 0, 0.0, flag)
+            passed = jnp.where(lane == LANES - 1, 0.0, flag)
+            image = [pltpu.roll(h * shown, brick, 1) + pltpu.roll(r * passed, brick + 1, 1)
+                     for h, r in zip(here, right)]
+            image.append(pltpu.roll((1.0 - clear) * shown, brick, 1))
+            leaving = lane == brick - 1
+            through = run_ref[3, rows, :]
+            done_ref[3, rows, :] = jnp.where(leaving, through, done_ref[3, rows, :])
+            through = jnp.where(leaving, 1.0, through)
+            for n in range(3):
+                sum_n = run_ref[n, rows, :]
+                done_ref[n, rows, :] = jnp.where(leaving, sum_n, done_ref[n, rows, :])
+                run_ref[n, rows, :] = jnp.where(leaving, 0.0, sum_n) + through * image[n]
+            run_ref[3, rows, :] = through - through * image[3]
         return carry
 
-    lax.fori_loop(0, bricks * groups, one, 0)
+    lax.fori_loop(0, bricks, one, 0)
 
     @pl.when(step == pl.num_programs(0) - 1)
     def _():
@@ -130,6 +168,8 @@
             pltpu.VMEM((8, GROUP, LANES), F32),
             pltpu.VMEM((4, rows, LANES), F32),
             pltpu.VMEM((4, rows, LANES), F32),
+            pltpu.VMEM((4, layers // STEPS, rows, LANES), F32),
+            pltpu.VMEM((8, KNOTS + 2, 8, LANES), F32),
         ],
         cost_estimate=pl.CostEstimate(flops=40_000_000, bytes_accessed=2_400_000, transcendentals=0),
         compiler_params=pltpu.CompilerParams(vmem_limit_bytes=32 * 1024 * 1024),
@@ -138,25 +178,27 @@
 
 
 def deal_kernel(flag_ref, color_ref, opacity_ref, column_ref, rim_ref, front_ref, tail_ref, out_ref,
-                pad_ref, table_ref, column_f32, rim_f32):
+                pad_ref, table_ref):
     build_tables(color_ref, opacity_ref, pad_ref, table_ref)
     tables = [table_ref[n] for n in range(8)]
     out_ref[...] = jnp.zeros_like(out_ref)
-    total, rows = column_ref.shape
-    bricks = total // BZ
+    rows = front_ref.shape[1]
+    beside = LANES // rows
+    bricks = column_ref.shape[0] * beside // BZ
     half = rows // 2
-    column_f32[:, 0:rows] = column_ref[...].astype(F32)
-    rim_f32[:, 0:rows] = rim_ref[...].astype(F32)
     start = lax.axis_index("gx") * LANES + lax.axis_index("gz") * bricks
     targets = out_ref.shape[0]
     lane = lane_ids(GROUP)
-    flags = jnp.broadcast_to(flag_ref[...].astype(F32), (bricks, LANES))
+    deep = lax.broadcasted_iota(jnp.int32, (bricks, LANES), 0)
+    flags = jnp.zeros((bricks, LANES), F32)
+    for b in range(bricks):
+        flags = jnp.where(deep == b, flag_ref[b].astype(F32), flags)
     to_alpha = lane % half + 3 * half
     for parity in range(2):
         spread = lane % half * 2 + parity
 
         def shaded(ref, k):
-            values = pick(ref[pl.ds(k, bricks, stride=BZ), :], spread)
+            values = pick(ref[pl.ds(k // beside, bricks, stride=BZ // beside), :], spread + k % beside * rows)
             red, green, blue, alpha = classify(values, tables)
             shade = jnp.where(lane < half, red, jnp.where(lane < 2 * half, green, blue))
             return alpha * jnp.where(lane < 3 * half, shade, 1.0), alpha
@@ -165,11 +207,11 @@
         clear = jnp.ones((bricks, LANES), F32)
         for k in range(BZ):
             f = k / BZ
-            sample, alpha = shaded(column_f32, k)
+            sample, alpha = shaded(column_ref, k)
             if k:
-                beside, beside_alpha = shaded(rim_f32, k)
-                sample = (1.0 - f) * sample + f * beside
-                alpha = (1.0 - f) * alpha + f * beside_alpha
+                left, left_alpha = shaded(rim_ref, k)
+                sample = (1.0 - f) * sample + f * left
+                alpha = (1.0 - f) * alpha + f * left_alpha
             image = image + clear * sample
             clear = clear - clear * alpha
         image = image * flags
@@ -184,14 +226,15 @@
 
 
 def deal(active, tf_color, tf_opacity, column, rim, front, tail, targets):
+    vmem = pl.BlockSpec(memory_space=pltpu.VMEM)
     return pl.pallas_call(
         deal_kernel,
+        in_specs=[pl.BlockSpec(memory_space=pltpu.SMEM)] + [vmem] * 6,
+        out_specs=vmem,
         out_shape=jax.ShapeDtypeStruct((targets, LANES), F32),
         scratch_shapes=[
             pltpu.VMEM((8, LANES), F32),
             pltpu.VMEM((8, GROUP, LANES), F32),
-            pltpu.VMEM((column.shape[0], LANES), F32),
-            pltpu.VMEM((column.shape[0], LANES), F32),
         ],
         compiler_params=pltpu.CompilerParams(vmem_limit_bytes=32 * 1024 * 1024),
         name="deal",
@@ -237,16 +280,42 @@
     )(arrived)
 
 
+def ends_kernel(volume_ref, first_ref, last_ref):
+    layers, rows, cols = volume_ref.shape
+    part = 16
+    row = lax.broadcasted_iota(jnp.int32, (16, cols), 0)
+    lane = lax.broadcasted_iota(jnp.int32, (16, cols), 1)
+    unit = jnp.where(lane == jnp.where(row == 0, 0, cols - 1), 1.0, 0.0).astype(jnp.bfloat16)
+    for start in range(0, layers, part):
+        cells = volume_ref[start:start + part].reshape(part * rows, cols)
+        both = lax.dot_general(unit, cells, (((1,), (1,)), ((), ())), preferred_element_type=F32)
+        first_ref[:, start * rows:(start + part) * rows] = both[0:1]
+        last_ref[:, start * rows:(start + part) * rows] = both[1:2]
+
+
+def ends(volume):
+    layers, rows, cols = volume.shape
+    out = jax.ShapeDtypeStruct((1, layers * rows), F32)
+    first, last = pl.pallas_call(
+        ends_kernel,
+        out_shape=[out, out],
+        compiler_params=pltpu.CompilerParams(vmem_limit_bytes=32 * 1024 * 1024),
+        name="ends",
+    )(volume)
+    return first.reshape(-1, LANES), last.reshape(-1, LANES)
+
+
 def body(volume, tf_color, tf_opacity, active):
     layers = volume.shape[0]
     bricks = layers // BZ
     across, down, depth = (lax.axis_size(name) for name in ("gx", "gy", "gz"))
     targets = across * down * depth
     opacity = tf_opacity.reshape(1, -1)
-    rim = lax.ppermute(volume[:, :, -1], "gx", [(i, i + 1) for i in range(across - 1)])
-    column = volume[:, :, 0]
-    front, tail = render(active, tf_color, opacity, volume)
-    rows = deal(active.reshape(bricks, 1), tf_color, opacity, column, rim, front, tail, targets)
+    flags = active.reshape(bricks)
+    column, last = ends(volume)
+    rim = lax.ppermute(last, "gx", [(i, i + 1) for i in range(across - 1)])
+    front, tail = render(flags, tf_color, opacity, volume)
+    rows = deal(flags, tf_color, opacity, column, rim, front, tail, targets)
     arrived = lax.all_to_all(rows, ("gx", "gy", "gz"), 0, 0, tiled=True)
     return gather(arrived, across, down, depth, bricks)
 

time: 107 us -> 78.1 us (0.73)
  Pallas kernels: 45.2 us -> 24.4 us
  local copies, waits for them, and re-layouts: 9.58 us -> 1.6 us
    pallas_call x1, Pallas kernels: 40.7 us -> 18.7 us  [render(): pl.pallas_call(render_kernel, grid=(STEPS,), in_specs=[pl.BlockSpec(memor...]
    slice x1 -> x0, local copies, waits for them, and re-layouts: 4.98 us -> none  [body(): volume[:, :, -1]]
    unnamed x11 -> x8, local copies, waits for them, and re-layouts: 4.52 us -> 1.6 us
    pallas_call x1 -> x2, Pallas kernels: 3.35 us -> 4.55 us  [the longest x1 3.9 us: deal(): pl.pallas_call(deal_kernel, in_specs=[pl.BlockSpec(memory_space=pltpu.SME...]
  transfers between devices with their start and end apart: 1 -> 1, of which waited for: 0 -> 0; matrix products, arithmetic and copies ran while one was open for 2% -> 0% of each run, Pallas kernels for 38% -> 24%
where the time goes in v2:
time: 78.1 us; the launch traced here: 78 us
  blocking collectives  48 us (61%)
  Pallas kernels  24.4 us (31%)
  starting transfers between devices  3.95 us (5%)
  local copies, waits for them, and re-layouts  1.6 us (2%)
    all_to_all x1, blocking collectives, body(): arrived = lax.all_to_all(rows, ('gx', 'gy', 'gz'), 0, 0, tiled=True)  48 us
    pallas_call x1, Pallas kernels, render(): pl.pallas_call(render_kernel, grid=(STEPS,), in_specs=[pl.BlockSpec(memor...  18.7 us
    ppermute x1, starting transfers between devices, body(): rim = lax.ppermute(last, 'gx', [(i, i + 1) for i in range(across - 1)])  3.95 us
    pallas_call x1, Pallas kernels, deal(): pl.pallas_call(deal_kernel, in_specs=[pl.BlockSpec(memory_space=pltpu.SME...  3.9 us
    unnamed x8, local copies, waits for them, and re-layouts  1.6 us
  transfers between devices with their start and end apart: 1, of which 0 were waited for; matrix products, arithmetic and copies ran while one was open for 0% of the time, Pallas kernels for 24%

profile of v2, /device:TPU:1, one launch (start us, length us, event | category | flops | bytes accessed | tf_op | source)
XLA Modules:
  0.0 78.0 jit_solution(3890094351903265099)
XLA Ops:
  0.0 0.0 copy-start
  0.0 1.6 %copy-done = bf16[128,64,128]{2,1,0:T(8,128)(2,1)S(1)} copy-done((bf16[128,64,128]{2,1,0:T(8,128)(2,1)S(1)}, bf16[128,64,128]{2,1,0:T(8,128)(2,1)}, u32[]{:S(2)}) %copy-start) | copy-done | bytes 2097176
  1.6 0.0 copy-start.1
  1.6 0.0 copy-start.2
  1.6 0.0 copy-start.3
  1.6 0.6 ends.1
  2.2 4.0 %collective-permute-start = (f32[64,128]{1,0:T(8,128)S(1)}, f32[64,128]{1,0:T(8,128)S(1)}, u32[]{:S(2)}, u32[]{:S(2)}) collective-permute-start(f32[64,128]{1,0:T(8,128)S(1)} %bitcast.15), channel_id=1, source_target_pairs={{0,128},{128,256},{256,384},{1,129},{129,257},{257,385},{2,130},{1... | collective-permute-start | bytes 98312 | tf_op jit(solution)/shard_map/ppermute | solution.py:316
  6.2 0.0 copy-done.1
  6.2 0.0 copy-done.2
  6.2 0.0 copy-done.3
  6.2 18.7 %render.1 = (f32[4,64,128]{2,1,0:T(8,128)S(1)}, f32[4,64,128]{2,1,0:T(8,128)S(1)}) custom-call(s32[16]{0:T(128)S(1)} %bitcast.11, f32[3,16]{1,0:T(4,128)S(1)} %copy-done.1, f32[1,16]{1,0:T(1,128)S(1)} %bitcast.13, bf16[128,64,128]{2,1,0:T(8,128)(2,1)S(1)} %copy-done), custom_call_target="tpu_custom_call" | custom-call | flops 40000000 | bytes 2400000 | tf_op jit(solution)/shard_map/render/pallas_call | solution.py:155
  24.9 0.0 collective-permute-done.rim_ref
  24.9 3.9 %deal.1 = f32[512,128]{1,0:T(8,128)S(1)} custom-call(s32[16]{0:T(128)S(1)} %bitcast.12, f32[3,16]{1,0:T(4,128)S(1)} %copy-done.1, f32[1,16]{1,0:T(1,128)S(1)} %bitcast.14, f32[64,128]{1,0:T(8,128)S(1)} %bitcast.10, f32[64,128]{1,0:T(8,128)S(1)} %collective-permute-done.rim_ref, f32[4,64,128]{2,1,0:T(8,128)S(1)} %get-tuple-element.11.front_ref, ...), custom_call_target="tpu_custom_call" | custom-call | tf_op jit(solution)/shard_map/deal/pallas_call | solution.py:230
  28.9 48.0 %all_to_all.11 = f32[512,1,128]{2,1,0:T(1,128)S(1)} all-to-all(f32[512,1,128]{2,1,0:T(1,128)S(1)} %bitcast.8), channel_id=1, replica_groups=mesh['gx'=4,'gy'=8,'gz'=16] {'gx','gy','gz'}, dimensions={0} | all-to-all | bytes 524288 | tf_op jit(solution)/shard_map/all_to_all | solution.py:319
  76.8 1.1 %gather.1 = f32[4,1,768]{2,1,0:T(1,128)} custom-call(f32[512,128]{1,0:T(8,128)S(1)} %bitcast.9), custom_call_target="tpu_custom_call" | custom-call | tf_op jit(solution)/shard_map/gather/pallas_call | solution.py:275
Async XLA Ops:
  0.0 1.6 %copy-start = (bf16[128,64,128]{2,1,0:T(8,128)(2,1)S(1)}, bf16[128,64,128]{2,1,0:T(8,128)(2,1)}, u32[]{:S(2)}) copy-start(bf16[128,64,128]{2,1,0:T(8,128)(2,1)} %volume_ref.3) | copy-start | bytes 6291460
  1.6 4.6 %copy-start.1 = (f32[3,16]{1,0:T(4,128)S(1)}, f32[3,16]{1,0:T(4,128)}, u32[]{:S(2)}) copy-start(f32[3,16]{1,0:T(4,128)} %color_ref.3) | copy-start | bytes 580
  1.6 4.6 %copy-start.2 = (s32[16,1,1]{0,2,1:T(1,128)S(1)}, s32[16,1,1]{0,2,1:T(1,128)}, u32[]{:S(2)}) copy-start(s32[16,1,1]{0,2,1:T(1,128)} %param.7) | copy-start | bytes 196
  1.6 4.6 %copy-start.3 = (f32[16]{0:T(128)S(1)}, f32[16]{0:T(128)}, u32[]{:S(2)}) copy-start(f32[16]{0:T(128)} %param.6) | copy-start | bytes 196
  2.2 22.7 %collective-permute-start = (f32[64,128]{1,0:T(8,128)S(1)}, f32[64,128]{1,0:T(8,128)S(1)}, u32[]{:S(2)}, u32[]{:S(2)}) collective-permute-start(f32[64,128]{1,0:T(8,128)S(1)} %bitcast.15), channel_id=1, source_target_pairs={{0,128},{128,256},{256,384},{1,129},{129,257},{257,385},{2,130},{1... | collective-permute-start | bytes 98312 | tf_op jit(solution)/shard_map/ppermute | solution.py:316

commit v3 on v2

--- a/solution.py
+++ b/solution.py
@@ -177,87 +177,117 @@
     )(active, tf_color, tf_opacity, volume)
 
 
+def rim_image(column_ref, rim_ref, flag_ref, tables, rows):
+    pairs = BZ * rows // LANES
+    bricks = column_ref.shape[0] // pairs
+    lane = lane_ids(bricks)
+    second = lane >= rows
+    deep = lax.broadcasted_iota(jnp.int32, (bricks, LANES), 0)
+    flags = jnp.zeros((bricks, LANES), F32)
+    for b in range(bricks):
+        flags = jnp.where(deep == b, flag_ref[b].astype(F32), flags)
+    image = [jnp.zeros((bricks, LANES), F32) for c in range(4)]
+    clear = jnp.ones((bricks, LANES), F32)
+    for pair in range(pairs):
+        f = jnp.where(second, (2 * pair + 1) / BZ, 2 * pair / BZ)
+        *own, alpha = classify(column_ref[pl.ds(pair, bricks, stride=pairs), :], tables)
+        *left, beside = classify(rim_ref[pl.ds(pair, bricks, stride=pairs), :], tables)
+        kept = (1.0 - f) * alpha
+        moved = f * beside
+        sample = [kept * a + moved * b for a, b in zip(own, left)] + [kept + moved]
+        for part in (sample, [pltpu.roll(value, rows, 1) for value in sample]):
+            image = [total + clear * value for total, value in zip(image, part)]
+            clear = clear - clear * part[3]
+    return [value * flags for value in image]
+
+
 def deal_kernel(flag_ref, color_ref, opacity_ref, column_ref, rim_ref, front_ref, tail_ref, out_ref,
                 pad_ref, table_ref):
     build_tables(color_ref, opacity_ref, pad_ref, table_ref)
     tables = [table_ref[n] for n in range(8)]
-    out_ref[...] = jnp.zeros_like(out_ref)
     rows = front_ref.shape[1]
-    beside = LANES // rows
-    bricks = column_ref.shape[0] * beside // BZ
     half = rows // 2
-    start = lax.axis_index("gx") * LANES + lax.axis_index("gz") * bricks
-    targets = out_ref.shape[0]
     lane = lane_ids(GROUP)
-    deep = lax.broadcasted_iota(jnp.int32, (bricks, LANES), 0)
-    flags = jnp.zeros((bricks, LANES), F32)
-    for b in range(bricks):
-        flags = jnp.where(deep == b, flag_ref[b].astype(F32), flags)
     to_alpha = lane % half + 3 * half
+    rim = rim_image(column_ref, rim_ref, flag_ref, tables, rows)
+    pieces = LANES // GROUP + 1
     for parity in range(2):
-        spread = lane % half * 2 + parity
-
-        def shaded(ref, k):
-            values = pick(ref[pl.ds(k // beside, bricks, stride=BZ // beside), :], spread + k % beside * rows)
-            red, green, blue, alpha = classify(values, tables)
-            shade = jnp.where(lane < half, red, jnp.where(lane < 2 * half, green, blue))
-            return alpha * jnp.where(lane < 3 * half, shade, 1.0), alpha
-
-        image = jnp.zeros((bricks, LANES), F32)
-        clear = jnp.ones((bricks, LANES), F32)
-        for k in range(BZ):
-            f = k / BZ
-            sample, alpha = shaded(column_ref, k)
-            if k:
-                left, left_alpha = shaded(rim_ref, k)
-                sample = (1.0 - f) * sample + f * left
-                alpha = (1.0 - f) * alpha + f * left_alpha
-            image = image + clear * sample
-            clear = clear - clear * alpha
-        image = image * flags
+        spread = [pick(value, lane % half * 2 + parity) for value in rim]
+        image = jnp.where(lane < half, spread[0], jnp.where(
+            lane < 2 * half, spread[1], jnp.where(lane < 3 * half, spread[2], spread[3])))
         near = jnp.concatenate([front_ref[n, pl.ds(parity, half, stride=2), :] for n in range(4)], axis=0).T
         far = jnp.concatenate([tail_ref[n, pl.ds(parity, half, stride=2), :] for n in range(4)], axis=0).T
-        for m in range(LANES // GROUP + 1):
-            place = lax.rem(start + parity * (targets // 2) + m * GROUP, targets)
-            piece = near[m * GROUP:(m + 1) * GROUP] if m < LANES // GROUP else far[:GROUP]
+        for m in range(pieces):
+            piece = near[m * GROUP:(m + 1) * GROUP] if m < pieces - 1 else far[:GROUP]
             if m == 0:
                 piece = piece + (1.0 - pick(piece, to_alpha)) * image
-            out_ref[pl.ds(pl.multiple_of(place, GROUP), GROUP), :] = piece
-
-
-def deal(active, tf_color, tf_opacity, column, rim, front, tail, targets):
+            out_ref[pl.ds(m * 2 + parity, GROUP, stride=2 * pieces), :] = piece
+
+
+def deal(flags, tf_color, tf_opacity, column, rim, front, tail):
     vmem = pl.BlockSpec(memory_space=pltpu.VMEM)
     return pl.pallas_call(
         deal_kernel,
         in_specs=[pl.BlockSpec(memory_space=pltpu.SMEM)] + [vmem] * 6,
         out_specs=vmem,
-        out_shape=jax.ShapeDtypeStruct((targets, LANES), F32),
+        out_shape=jax.ShapeDtypeStruct((2 * (LANES + GROUP), LANES), F32),
         scratch_shapes=[
             pltpu.VMEM((8, LANES), F32),
             pltpu.VMEM((8, GROUP, LANES), F32),
         ],
         compiler_params=pltpu.CompilerParams(vmem_limit_bytes=32 * 1024 * 1024),
         name="deal",
-    )(active, tf_color, tf_opacity, column, rim, front, tail)
-
-
-def gather_kernel(across, down, depth, bricks, arrived_ref, out_ref):
-    targets = across * down * depth
-    me = (lax.axis_index("gx") * down + lax.axis_index("gy")) * depth + lax.axis_index("gz")
+    )(flags, tf_color, tf_opacity, column, rim, front, tail)
+
+
+def along_depth_kernel(across, down, depth, arrived_ref, out_ref, total_ref, clear_ref):
+    taken = arrived_ref.shape[0] // depth
+    total_ref[...] = jnp.zeros_like(total_ref)
+    clear_ref[...] = jnp.ones_like(clear_ref)
+    quarter = LANES // 4
+    lane = lane_ids(taken)
+    to_alpha = lane % quarter + 3 * quarter
+    for z in range(depth):
+        piece = arrived_ref[z * taken:(z + 1) * taken, :]
+        alpha = pick(piece, to_alpha)
+        place = slice(2 * z, 2 * z + taken)
+        clear = clear_ref[place, :]
+        total_ref[place, :] = total_ref[place, :] + clear * piece
+        clear_ref[place, :] = clear - clear * alpha
+    span = 2 * down
+    even = lax.broadcasted_iota(jnp.int32, (span, LANES), 0) % 2 == 0
+    blocks = [total_ref[q * span:(q + 1) * span, :] for q in range(3)]
+    blocks.append(jnp.zeros((span, LANES), F32))
+    x = lax.axis_index("gx")
+    for q in range(across):
+        place = lax.rem(x + q, across) * span
+        out_ref[pl.ds(pl.multiple_of(place, span), span), :] = jnp.where(even, blocks[q], blocks[(q + 2) % 4])
+
+
+def along_depth(arrived, across, down, depth):
+    return pl.pallas_call(
+        functools.partial(along_depth_kernel, across, down, depth),
+        out_shape=jax.ShapeDtypeStruct((across * down * 2, LANES), F32),
+        scratch_shapes=[pltpu.VMEM((6 * down, LANES), F32), pltpu.VMEM((6 * down, LANES), F32)],
+        compiler_params=pltpu.CompilerParams(vmem_limit_bytes=32 * 1024 * 1024),
+        name="along_depth",
+    )(arrived)
+
+
+def gather_kernel(across, down, arrived_ref, out_ref):
+    me = lax.axis_index("gx")
     half = LANES // 4
     lane = lane_ids(down)
     to_alpha = lane % half + 3 * half
     total = [jnp.zeros((down, LANES), F32) for k in range(3)]
     clear = [jnp.ones((down, LANES), F32) for k in range(3)]
-    for front in range(depth):
-        for x in reversed(range(across)):
-            start = x * LANES + front * bricks
-            behind = lax.rem(me - start + 2 * targets, targets)
-            slot = jnp.where(me < start, 1, 0) + jnp.where(behind >= targets // 2, 1, 0)
-            piece = arrived_ref[pl.ds(x * down * depth + front, down, stride=depth), :]
+    for x in reversed(range(across)):
+        slots = (jnp.where(me < x, 1, 0), jnp.where(me >= x + 2, 1, 2))
+        for parity in range(2):
+            piece = arrived_ref[pl.ds(x * 2 * down + parity, down, stride=2), :]
             alpha = pick(piece, to_alpha)
-            for k in range(3):
-                mine = jnp.where(slot == k, 1.0, 0.0)
+            for k in range(2) if parity == 0 else range(1, 3):
+                mine = jnp.where(slots[parity] == k, 1.0, 0.0)
                 total[k] = total[k] + clear[k] * (piece * mine)
                 clear[k] = clear[k] - clear[k] * (alpha * mine)
     width = 3 * half
@@ -270,10 +300,10 @@
             out_ref[c, 0:1, y * width:(y + 1) * width] = row[y:y + 1, 0:width]
 
 
-def gather(arrived, across, down, depth, bricks):
+def gather(arrived, across, down):
     pixels = down * 3 * LANES // 4
     return pl.pallas_call(
-        functools.partial(gather_kernel, across, down, depth, bricks),
+        functools.partial(gather_kernel, across, down),
         out_shape=jax.ShapeDtypeStruct((4, 1, pixels), F32),
         compiler_params=pltpu.CompilerParams(vmem_limit_bytes=32 * 1024 * 1024),
         name="gather",
@@ -309,15 +339,16 @@
     layers = volume.shape[0]
     bricks = layers // BZ
     across, down, depth = (lax.axis_size(name) for name in ("gx", "gy", "gz"))
-    targets = across * down * depth
     opacity = tf_opacity.reshape(1, -1)
     flags = active.reshape(bricks)
     column, last = ends(volume)
     rim = lax.ppermute(last, "gx", [(i, i + 1) for i in range(across - 1)])
     front, tail = render(flags, tf_color, opacity, volume)
-    rows = deal(flags, tf_color, opacity, column, rim, front, tail, targets)
-    arrived = lax.all_to_all(rows, ("gx", "gy", "gz"), 0, 0, tiled=True)
-    return gather(arrived, across, down, depth, bricks)
+    rows = deal(flags, tf_color, opacity, column, rim, front, tail)
+    swapped = lax.all_to_all(rows.reshape(depth, 1, -1), "gz", 0, 0, tiled=True)
+    merged = along_depth(swapped.reshape(-1, LANES), across, down, depth)
+    arrived = lax.all_to_all(merged.reshape(across * down, 1, -1), ("gx", "gy"), 0, 0, tiled=True)
+    return gather(arrived.reshape(-1, LANES), across, down)
 
 
 def solution(mesh):

time: 78.1 us -> 72.2 us (0.924)
  blocking collectives: 48 us -> 44.7 us
  Pallas kernels: 24.4 us -> 21.7 us
    all_to_all x1 -> x2, blocking collectives: 48 us -> 44.7 us  [the longest x1 26.8 us: body(): swapped = lax.all_to_all(rows.reshape(depth, 1, -1), 'gz', 0, 0, tiled=True)]
    pallas_call x1, Pallas kernels: 3.9 us -> 1.34 us  [deal(): pl.pallas_call(deal_kernel, in_specs=[pl.BlockSpec(memory_space=pltpu.SME...]
  transfers between devices with their start and end apart: 1 -> 1, of which waited for: 0 -> 0; matrix products, arithmetic and copies ran while one was open for 0% -> 0% of each run, Pallas kernels for 24% -> 26%
where the time goes in v3:
time: 72.2 us; the launch traced here: 72 us
  blocking collectives  44.7 us (62%)
  Pallas kernels  21.7 us (30%)
  starting transfers between devices  3.95 us (5%)
  local copies, waits for them, and re-layouts  1.6 us (2%)
    all_to_all x1, blocking collectives, body(): swapped = lax.all_to_all(rows.reshape(depth, 1, -1), 'gz', 0, 0, tiled=True)  26.8 us
    pallas_call x1, Pallas kernels, render(): pl.pallas_call(render_kernel, grid=(STEPS,), in_specs=[pl.BlockSpec(memor...  18.7 us
    all_to_all x1, blocking collectives, body(): lax.all_to_all(merged.reshape(across * down, 1, -1), ('gx', 'gy'), 0, 0,...  17.9 us
    ppermute x1, starting transfers between devices, body(): rim = lax.ppermute(last, 'gx', [(i, i + 1) for i in range(across - 1)])  3.95 us
    unnamed x8, local copies, waits for them, and re-layouts  1.6 us
  transfers between devices with their start and end apart: 1, of which 0 were waited for; matrix products, arithmetic and copies ran while one was open for 0% of the time, Pallas kernels for 26%

profile of v3, /device:TPU:1, one launch (start us, length us, event | category | flops | bytes accessed | tf_op | source)
XLA Modules:
  0.0 72.0 jit_solution(11632362862462750283)
XLA Ops:
  0.0 0.0 copy-start
  0.0 1.6 %copy-done = bf16[128,64,128]{2,1,0:T(8,128)(2,1)S(1)} copy-done((bf16[128,64,128]{2,1,0:T(8,128)(2,1)S(1)}, bf16[128,64,128]{2,1,0:T(8,128)(2,1)}, u32[]{:S(2)}) %copy-start) | copy-done | bytes 2097176
  1.6 0.0 copy-start.1
  1.6 0.0 copy-start.2
  1.6 0.0 copy-start.3
  1.6 0.6 ends.1
  2.2 4.0 %collective-permute-start = (f32[64,128]{1,0:T(8,128)S(1)}, f32[64,128]{1,0:T(8,128)S(1)}, u32[]{:S(2)}, u32[]{:S(2)}) collective-permute-start(f32[64,128]{1,0:T(8,128)S(1)} %bitcast.17), channel_id=1, source_target_pairs={{0,128},{128,256},{256,384},{1,129},{129,257},{257,385},{2,130},{1... | collective-permute-start | bytes 98312 | tf_op jit(solution)/shard_map/ppermute | solution.py:345
  6.2 0.0 copy-done.1
  6.2 0.0 copy-done.2
  6.2 0.0 copy-done.3
  6.2 18.7 %render.1 = (f32[4,64,128]{2,1,0:T(8,128)S(1)}, f32[4,64,128]{2,1,0:T(8,128)S(1)}) custom-call(s32[16]{0:T(128)S(1)} %bitcast.13, f32[3,16]{1,0:T(4,128)S(1)} %copy-done.1, f32[1,16]{1,0:T(1,128)S(1)} %bitcast.15, bf16[128,64,128]{2,1,0:T(8,128)(2,1)S(1)} %copy-done), custom_call_target="tpu_custom_call" | custom-call | flops 40000000 | bytes 2400000 | tf_op jit(solution)/shard_map/render/pallas_call | solution.py:155
  24.9 0.0 collective-permute-done.rim_ref
  24.9 1.3 %deal.1 = f32[288,128]{1,0:T(8,128)S(1)} custom-call(s32[16]{0:T(128)S(1)} %bitcast.14, f32[3,16]{1,0:T(4,128)S(1)} %copy-done.1, f32[1,16]{1,0:T(1,128)S(1)} %bitcast.16, f32[64,128]{1,0:T(8,128)S(1)} %bitcast.12, f32[64,128]{1,0:T(8,128)S(1)} %collective-permute-done.rim_ref, f32[4,64,128]{2,1,0:T(8,128)S(1)} %get-tuple-element.11.front_ref, ...), custom_call_target="tpu_custom_call" | custom-call | tf_op jit(solution)/shard_map/deal/pallas_call | solution.py:229
  26.3 26.8 %all_to_all.10 = f32[16,1,2304]{2,1,0:T(1,128)S(1)} all-to-all(f32[16,1,2304]{2,1,0:T(1,128)S(1)} %bitcast.9), channel_id=1, replica_groups=mesh['gx'=4,'gy'=8,'gz'=16] {'gz'}, dimensions={0} | all-to-all | bytes 294912 | tf_op jit(solution)/shard_map/all_to_all | solution.py:348
  53.1 0.2 along_depth.1
  53.3 17.9 %all_to_all.11 = f32[32,1,256]{2,1,0:T(1,128)S(1)} all-to-all(f32[32,1,256]{2,1,0:T(1,128)S(1)} %bitcast.11), channel_id=1, replica_groups=mesh['gx'=4,'gy'=8,'gz'=16] {'gx','gy'}, dimensions={0} | all-to-all | bytes 65536 | tf_op jit(solution)/shard_map/all_to_all | solution.py:350
  71.2 0.9 %gather.1 = f32[4,1,768]{2,1,0:T(1,128)} custom-call(f32[64,128]{1,0:T(8,128)S(1)} %bitcast.10), custom_call_target="tpu_custom_call" | custom-call | tf_op jit(solution)/shard_map/gather/pallas_call | solution.py:305
Async XLA Ops:
  0.0 1.6 %copy-start = (bf16[128,64,128]{2,1,0:T(8,128)(2,1)S(1)}, bf16[128,64,128]{2,1,0:T(8,128)(2,1)}, u32[]{:S(2)}) copy-start(bf16[128,64,128]{2,1,0:T(8,128)(2,1)} %volume_ref.3) | copy-start | bytes 6291460
  1.6 4.6 %copy-start.1 = (f32[3,16]{1,0:T(4,128)S(1)}, f32[3,16]{1,0:T(4,128)}, u32[]{:S(2)}) copy-start(f32[3,16]{1,0:T(4,128)} %color_ref.3) | copy-start | bytes 580
  1.6 4.6 %copy-start.2 = (s32[16,1,1]{0,2,1:T(1,128)S(1)}, s32[16,1,1]{0,2,1:T(1,128)}, u32[]{:S(2)}) copy-start(s32[16,1,1]{0,2,1:T(1,128)} %param.7) | copy-start | bytes 196
  1.6 4.6 %copy-start.3 = (f32[16]{0:T(128)S(1)}, f32[16]{0:T(128)}, u32[]{:S(2)}) copy-start(f32[16]{0:T(128)} %param.6) | copy-start | bytes 196
  2.2 22.7 %collective-permute-start = (f32[64,128]{1,0:T(8,128)S(1)}, f32[64,128]{1,0:T(8,128)S(1)}, u32[]{:S(2)}, u32[]{:S(2)}) collective-permute-start(f32[64,128]{1,0:T(8,128)S(1)} %bitcast.17), channel_id=1, source_target_pairs={{0,128},{128,256},{256,384},{1,129},{129,257},{257,385},{2,130},{1... | collective-permute-start | bytes 98312 | tf_op jit(solution)/shard_map/ppermute | solution.py:345

commit v4 on v3

--- a/solution.py
+++ b/solution.py
@@ -24,6 +24,30 @@
 
 def pick(table, index):
     return jnp.take_along_axis(table, index, axis=1, mode="promise_in_bounds")
+
+
+def code_step(opacity, layers):
+    clear = 1.0 - jnp.max(opacity, axis=1, keepdims=True)
+    left = jnp.ones_like(clear)
+    while layers:
+        if layers % 2:
+            left = left * clear
+        clear = clear * clear
+        layers //= 2
+    return (1.0 - left) * (1.0 / 65500.0)
+
+
+def pack(even, odd, step):
+    per = 1.0 / step
+    low = (even * per + 0.5).astype(jnp.int32)
+    high = (odd * per + 0.5).astype(jnp.int32)
+    return lax.shift_left(high, 16) | low
+
+
+def unpack(word, step):
+    low = (word & 0xFFFF).astype(F32) * step
+    high = lax.shift_right_logical(word, 16).astype(F32) * step
+    return low, high
 
 
 def build_tables(color_ref, opacity_ref, pad_ref, table_ref):
@@ -201,36 +225,38 @@
     return [value * flags for value in image]
 
 
-def deal_kernel(flag_ref, color_ref, opacity_ref, column_ref, rim_ref, front_ref, tail_ref, out_ref,
+def deal_kernel(layers, flag_ref, color_ref, opacity_ref, column_ref, rim_ref, front_ref, tail_ref, out_ref,
                 pad_ref, table_ref):
     build_tables(color_ref, opacity_ref, pad_ref, table_ref)
     tables = [table_ref[n] for n in range(8)]
+    step = code_step(opacity_ref[...], layers)
     rows = front_ref.shape[1]
     half = rows // 2
     lane = lane_ids(GROUP)
     to_alpha = lane % half + 3 * half
     rim = rim_image(column_ref, rim_ref, flag_ref, tables, rows)
     pieces = LANES // GROUP + 1
+    near, far, image = [], [], []
     for parity in range(2):
         spread = [pick(value, lane % half * 2 + parity) for value in rim]
-        image = jnp.where(lane < half, spread[0], jnp.where(
-            lane < 2 * half, spread[1], jnp.where(lane < 3 * half, spread[2], spread[3])))
-        near = jnp.concatenate([front_ref[n, pl.ds(parity, half, stride=2), :] for n in range(4)], axis=0).T
-        far = jnp.concatenate([tail_ref[n, pl.ds(parity, half, stride=2), :] for n in range(4)], axis=0).T
-        for m in range(pieces):
-            piece = near[m * GROUP:(m + 1) * GROUP] if m < pieces - 1 else far[:GROUP]
-            if m == 0:
-                piece = piece + (1.0 - pick(piece, to_alpha)) * image
-            out_ref[pl.ds(m * 2 + parity, GROUP, stride=2 * pieces), :] = piece
-
-
-def deal(flags, tf_color, tf_opacity, column, rim, front, tail):
+        image.append(jnp.where(lane < half, spread[0], jnp.where(
+            lane < 2 * half, spread[1], jnp.where(lane < 3 * half, spread[2], spread[3]))))
+        near.append(jnp.concatenate([front_ref[n, pl.ds(parity, half, stride=2), :] for n in range(4)], axis=0).T)
+        far.append(jnp.concatenate([tail_ref[n, pl.ds(parity, half, stride=2), :] for n in range(4)], axis=0).T)
+    for m in range(pieces):
+        pair = [n[m * GROUP:(m + 1) * GROUP] if m < pieces - 1 else f[:GROUP] for n, f in zip(near, far)]
+        if m == 0:
+            pair = [piece + (1.0 - pick(piece, to_alpha)) * late for piece, late in zip(pair, image)]
+        out_ref[pl.ds(m, GROUP, stride=pieces), :] = pack(*pair, step)
+
+
+def deal(layers, flags, tf_color, tf_opacity, column, rim, front, tail):
     vmem = pl.BlockSpec(memory_space=pltpu.VMEM)
     return pl.pallas_call(
-        deal_kernel,
+        functools.partial(deal_kernel, layers),
         in_specs=[pl.BlockSpec(memory_space=pltpu.SMEM)] + [vmem] * 6,
         out_specs=vmem,
-        out_shape=jax.ShapeDtypeStruct((2 * (LANES + GROUP), LANES), F32),
+        out_shape=jax.ShapeDtypeStruct((LANES + GROUP, LANES), jnp.int32),
         scratch_shapes=[
             pltpu.VMEM((8, LANES), F32),
             pltpu.VMEM((8, GROUP, LANES), F32),
@@ -240,41 +266,43 @@
     )(flags, tf_color, tf_opacity, column, rim, front, tail)
 
 
-def along_depth_kernel(across, down, depth, arrived_ref, out_ref, total_ref, clear_ref):
+def along_depth_kernel(across, down, depth, layers, opacity_ref, arrived_ref, out_ref, total_ref, clear_ref):
     taken = arrived_ref.shape[0] // depth
+    step = code_step(opacity_ref[...], layers)
     total_ref[...] = jnp.zeros_like(total_ref)
     clear_ref[...] = jnp.ones_like(clear_ref)
     quarter = LANES // 4
     lane = lane_ids(taken)
     to_alpha = lane % quarter + 3 * quarter
     for z in range(depth):
-        piece = arrived_ref[z * taken:(z + 1) * taken, :]
-        alpha = pick(piece, to_alpha)
-        place = slice(2 * z, 2 * z + taken)
-        clear = clear_ref[place, :]
-        total_ref[place, :] = total_ref[place, :] + clear * piece
-        clear_ref[place, :] = clear - clear * alpha
-    span = 2 * down
-    even = lax.broadcasted_iota(jnp.int32, (span, LANES), 0) % 2 == 0
-    blocks = [total_ref[q * span:(q + 1) * span, :] for q in range(3)]
-    blocks.append(jnp.zeros((span, LANES), F32))
+        place = slice(z, z + taken)
+        for parity, piece in enumerate(unpack(arrived_ref[z * taken:(z + 1) * taken, :], step)):
+            alpha = pick(piece, to_alpha)
+            clear = clear_ref[parity, place, :]
+            total_ref[parity, place, :] = total_ref[parity, place, :] + clear * piece
+            clear_ref[parity, place, :] = clear - clear * alpha
+    blocks = [[total_ref[parity, q * down:(q + 1) * down, :] for q in range(3)] for parity in range(2)]
+    empty = jnp.zeros((down, LANES), F32)
+    even, odd = blocks[0] + [empty], blocks[1] + [empty]
+    step = code_step(opacity_ref[...], layers * depth)
     x = lax.axis_index("gx")
     for q in range(across):
-        place = lax.rem(x + q, across) * span
-        out_ref[pl.ds(pl.multiple_of(place, span), span), :] = jnp.where(even, blocks[q], blocks[(q + 2) % 4])
-
-
-def along_depth(arrived, across, down, depth):
+        place = lax.rem(x + q, across) * down
+        out_ref[pl.ds(pl.multiple_of(place, down), down), :] = pack(even[q], odd[(q + 2) % 4], step)
+
+
+def along_depth(layers, tf_opacity, arrived, across, down, depth):
     return pl.pallas_call(
-        functools.partial(along_depth_kernel, across, down, depth),
-        out_shape=jax.ShapeDtypeStruct((across * down * 2, LANES), F32),
-        scratch_shapes=[pltpu.VMEM((6 * down, LANES), F32), pltpu.VMEM((6 * down, LANES), F32)],
+        functools.partial(along_depth_kernel, across, down, depth, layers),
+        out_shape=jax.ShapeDtypeStruct((across * down, LANES), jnp.int32),
+        scratch_shapes=[pltpu.VMEM((2, 3 * down, LANES), F32), pltpu.VMEM((2, 3 * down, LANES), F32)],
         compiler_params=pltpu.CompilerParams(vmem_limit_bytes=32 * 1024 * 1024),
         name="along_depth",
-    )(arrived)
-
-
-def gather_kernel(across, down, arrived_ref, out_ref):
+    )(tf_opacity, arrived)
+
+
+def gather_kernel(across, down, layers, opacity_ref, arrived_ref, out_ref):
+    step = code_step(opacity_ref[...], layers)
     me = lax.axis_index("gx")
     half = LANES // 4
     lane = lane_ids(down)
@@ -283,8 +311,7 @@
     clear = [jnp.ones((down, LANES), F32) for k in range(3)]
     for x in reversed(range(across)):
         slots = (jnp.where(me < x, 1, 0), jnp.where(me >= x + 2, 1, 2))
-        for parity in range(2):
-            piece = arrived_ref[pl.ds(x * 2 * down + parity, down, stride=2), :]
+        for parity, piece in enumerate(unpack(arrived_ref[x * down:(x + 1) * down, :], step)):
             alpha = pick(piece, to_alpha)
             for k in range(2) if parity == 0 else range(1, 3):
                 mine = jnp.where(slots[parity] == k, 1.0, 0.0)
@@ -300,14 +327,14 @@
             out_ref[c, 0:1, y * width:(y + 1) * width] = row[y:y + 1, 0:width]
 
 
-def gather(arrived, across, down):
+def gather(layers, tf_opacity, arrived, across, down):
     pixels = down * 3 * LANES // 4
     return pl.pallas_call(
-        functools.partial(gather_kernel, across, down),
+        functools.partial(gather_kernel, across, down, layers),
         out_shape=jax.ShapeDtypeStruct((4, 1, pixels), F32),
         compiler_params=pltpu.CompilerParams(vmem_limit_bytes=32 * 1024 * 1024),
         name="gather",
-    )(arrived)
+    )(tf_opacity, arrived)
 
 
 def ends_kernel(volume_ref, first_ref, last_ref):
@@ -344,11 +371,11 @@
     column, last = ends(volume)
     rim = lax.ppermute(last, "gx", [(i, i + 1) for i in range(across - 1)])
     front, tail = render(flags, tf_color, opacity, volume)
-    rows = deal(flags, tf_color, opacity, column, rim, front, tail)
+    rows = deal(layers, flags, tf_color, opacity, column, rim, front, tail)
     swapped = lax.all_to_all(rows.reshape(depth, 1, -1), "gz", 0, 0, tiled=True)
-    merged = along_depth(swapped.reshape(-1, LANES), across, down, depth)
+    merged = along_depth(layers, opacity, swapped.reshape(-1, LANES), across, down, depth)
     arrived = lax.all_to_all(merged.reshape(across * down, 1, -1), ("gx", "gy"), 0, 0, tiled=True)
-    return gather(arrived.reshape(-1, LANES), across, down)
+    return gather(layers * depth, opacity, arrived.reshape(-1, LANES), across, down)
 
 
 def solution(mesh):

time: 72.2 us -> 70.1 us (0.971)
  blocking collectives: 44.7 us -> 42.3 us
    all_to_all x1, blocking collectives: 17.9 us -> 15.8 us  [body(): lax.all_to_all(merged.reshape(across * down, 1, -1), ('gx', 'gy'), 0, 0,...]
  transfers between devices with their start and end apart: 1 -> 1, of which waited for: 0 -> 0; matrix products, arithmetic and copies ran while one was open for 0% -> 0% of each run, Pallas kernels for 26% -> 27%
where the time goes in v4:
time: 70.1 us; the launch traced here: 69.9 us
  blocking collectives  42.3 us (60%)
  Pallas kernels  22 us (31%)
  starting transfers between devices  3.95 us (6%)
  local copies, waits for them, and re-layouts  1.6 us (2%)
    all_to_all x1, blocking collectives, body(): swapped = lax.all_to_all(rows.reshape(depth, 1, -1), 'gz', 0, 0, tiled=True)  26.4 us
    pallas_call x1, Pallas kernels, render(): pl.pallas_call(render_kernel, grid=(STEPS,), in_specs=[pl.BlockSpec(memor...  18.7 us
    all_to_all x1, blocking collectives, body(): lax.all_to_all(merged.reshape(across * down, 1, -1), ('gx', 'gy'), 0, 0,...  15.8 us
    ppermute x1, starting transfers between devices, body(): rim = lax.ppermute(last, 'gx', [(i, i + 1) for i in range(across - 1)])  3.95 us
    unnamed x8, local copies, waits for them, and re-layouts  1.6 us
    pallas_call x1, Pallas kernels, deal(): pl.pallas_call(functools.partial(deal_kernel, layers), in_specs=[pl.Block...  1.44 us
  transfers between devices with their start and end apart: 1, of which 0 were waited for; matrix products, arithmetic and copies ran while one was open for 0% of the time, Pallas kernels for 27%

profile of v4, /device:TPU:1, one launch (start us, length us, event | category | flops | bytes accessed | tf_op | source)
XLA Modules:
  0.0 69.9 jit_solution(14689750531154314671)
XLA Ops:
  0.0 0.0 copy-start
  0.0 1.6 %copy-done = bf16[128,64,128]{2,1,0:T(8,128)(2,1)S(1)} copy-done((bf16[128,64,128]{2,1,0:T(8,128)(2,1)S(1)}, bf16[128,64,128]{2,1,0:T(8,128)(2,1)}, u32[]{:S(2)}) %copy-start) | copy-done | bytes 2097176
  1.6 0.0 copy-start.1
  1.6 0.0 copy-start.2
  1.6 0.0 copy-start.3
  1.6 0.6 ends.1
  2.2 4.0 %collective-permute-start = (f32[64,128]{1,0:T(8,128)S(1)}, f32[64,128]{1,0:T(8,128)S(1)}, u32[]{:S(2)}, u32[]{:S(2)}) collective-permute-start(f32[64,128]{1,0:T(8,128)S(1)} %bitcast.21), channel_id=1, source_target_pairs={{0,128},{128,256},{256,384},{1,129},{129,257},{257,385},{2,130},{1... | collective-permute-start | bytes 98312 | tf_op jit(solution)/shard_map/ppermute | solution.py:372
  6.2 0.0 copy-done.1
  6.2 0.0 copy-done.2
  6.2 0.0 copy-done.3
  6.2 18.7 %render.1 = (f32[4,64,128]{2,1,0:T(8,128)S(1)}, f32[4,64,128]{2,1,0:T(8,128)S(1)}) custom-call(s32[16]{0:T(128)S(1)} %bitcast.19, f32[3,16]{1,0:T(4,128)S(1)} %copy-done.1, f32[1,16]{1,0:T(1,128)S(1)} %bitcast.15, bf16[128,64,128]{2,1,0:T(8,128)(2,1)S(1)} %copy-done), custom_call_target="tpu_custom_call" | custom-call | flops 40000000 | bytes 2400000 | tf_op jit(solution)/shard_map/render/pallas_call | solution.py:179
  24.9 0.0 collective-permute-done.rim_ref
  24.9 1.4 %deal.1 = s32[144,128]{1,0:T(8,128)S(1)} custom-call(s32[16]{0:T(128)S(1)} %bitcast.20, f32[3,16]{1,0:T(4,128)S(1)} %copy-done.1, f32[1,16]{1,0:T(1,128)S(1)} %bitcast.16, f32[64,128]{1,0:T(8,128)S(1)} %bitcast.14, f32[64,128]{1,0:T(8,128)S(1)} %collective-permute-done.rim_ref, f32[4,64,128]{2,1,0:T(8,128)S(1)} %get-tuple-element.11.front_ref, ...), custom_call_target="tpu_custom_call" | custom-call | tf_op jit(solution)/shard_map/deal/pallas_call | solution.py:255
  26.4 26.4 %all_to_all.10 = s32[16,1,1152]{2,1,0:T(1,128)S(1)} all-to-all(s32[16,1,1152]{2,1,0:T(1,128)S(1)} %bitcast.11), channel_id=1, replica_groups=mesh['gx'=4,'gy'=8,'gz'=16] {'gz'}, dimensions={0} | all-to-all | bytes 147456 | tf_op jit(solution)/shard_map/all_to_all | solution.py:375
  52.8 0.3 along_depth.1
  53.1 15.8 %all_to_all.11 = s32[32,1,128]{2,1,0:T(1,128)S(1)} all-to-all(s32[32,1,128]{2,1,0:T(1,128)S(1)} %bitcast.13), channel_id=1, replica_groups=mesh['gx'=4,'gy'=8,'gz'=16] {'gx','gy'}, dimensions={0} | all-to-all | bytes 32768 | tf_op jit(solution)/shard_map/all_to_all | solution.py:377
  69.0 1.0 %gather.1 = f32[4,1,768]{2,1,0:T(1,128)} custom-call(f32[1,16]{1,0:T(1,128)S(1)} %bitcast.18, s32[32,128]{1,0:T(8,128)S(1)} %bitcast.12), custom_call_target="tpu_custom_call" | custom-call | tf_op jit(solution)/shard_map/gather/pallas_call | solution.py:332
Async XLA Ops:
  0.0 1.6 %copy-start = (bf16[128,64,128]{2,1,0:T(8,128)(2,1)S(1)}, bf16[128,64,128]{2,1,0:T(8,128)(2,1)}, u32[]{:S(2)}) copy-start(bf16[128,64,128]{2,1,0:T(8,128)(2,1)} %volume_ref.3) | copy-start | bytes 6291460
  1.6 4.6 %copy-start.1 = (f32[3,16]{1,0:T(4,128)S(1)}, f32[3,16]{1,0:T(4,128)}, u32[]{:S(2)}) copy-start(f32[3,16]{1,0:T(4,128)} %color_ref.3) | copy-start | bytes 580
  1.6 4.6 %copy-start.2 = (f32[16]{0:T(128)S(1)}, f32[16]{0:T(128)}, u32[]{:S(2)}) copy-start(f32[16]{0:T(128)} %param.6) | copy-start | bytes 196
  1.6 4.6 %copy-start.3 = (s32[16,1,1]{0,2,1:T(1,128)S(1)}, s32[16,1,1]{0,2,1:T(1,128)}, u32[]{:S(2)}) copy-start(s32[16,1,1]{0,2,1:T(1,128)} %param.7) | copy-start | bytes 196
  2.2 22.7 %collective-permute-start = (f32[64,128]{1,0:T(8,128)S(1)}, f32[64,128]{1,0:T(8,128)S(1)}, u32[]{:S(2)}, u32[]{:S(2)}) collective-permute-start(f32[64,128]{1,0:T(8,128)S(1)} %bitcast.21), channel_id=1, source_target_pairs={{0,128},{128,256},{256,384},{1,129},{129,257},{257,385},{2,130},{1... | collective-permute-start | bytes 98312 | tf_op jit(solution)/shard_map/ppermute | solution.py:372

commit v5 on v4

--- a/solution.py
+++ b/solution.py
@@ -14,7 +14,6 @@
 GROUP = 16
 STEPS = 4
 UNROLL = 4
-CHAINED = (2, 5)
 F32 = jnp.float32
 
 
@@ -54,39 +53,44 @@
     pad_ref[...] = jnp.zeros_like(pad_ref)
     pad_ref[0:3, 0:KNOTS] = color_ref[...]
     pad_ref[3:4, 0:KNOTS] = opacity_ref[...]
-    upper = pad_ref[...]
-    lower = pltpu.roll(upper, 1, 1)
-    slope = upper - lower
-    base = lower - slope * lane_ids(8).astype(F32)
-    for n in range(4):
-        table_ref[n] = jnp.broadcast_to(base[n:n + 1], (GROUP, LANES))
-        table_ref[4 + n] = jnp.broadcast_to(slope[n:n + 1], (GROUP, LANES))
+    knots = pad_ref[...]
+    lane = lane_ids(8)
+    slope = jnp.where(lane < KNOTS - 1, pltpu.roll(knots, LANES - 1, 1) - knots, 0.0)
+    base = knots - slope * lane.astype(F32)
+    row = lax.broadcasted_iota(jnp.int32, (8, LANES), 0)
+    for half in range(2):
+        for n in range(4):
+            for m, source in enumerate((base, slope)):
+                spread = jnp.broadcast_to(source[n:n + 1], (8, LANES))
+                table_ref[half, m * 4 + n] = pick(spread, row + 8 * half)
+
+
+def read_tables(table_ref):
+    return [[table_ref[half, n] for n in range(8)] for half in range(2)]
 
 
 def classify(values, tables):
     scale = (KNOTS - 1) / (2.0 * LIMIT)
-    place = jnp.clip(values * scale + (LIMIT * scale + 1.0), 0.0, KNOTS + 1.0)
-    index = place.astype(jnp.int32)
-    got = [pick(table, index) for table in tables]
-    return [got[n] + got[4 + n] * place for n in range(4)]
-
-
-def climb(values, knot_ref):
-    scale = (KNOTS - 1) / (2.0 * LIMIT)
-    place = values * scale + (LIMIT * scale + 1.0)
-    base = [jnp.zeros_like(values) for n in range(4)]
-    slope = [knot_ref[4 + n, 0] for n in range(4)]
-    for k in range(KNOTS + 2):
-        above = place >= float(k)
-        for n in range(4):
-            if k:
-                base[n] = jnp.where(above, knot_ref[n, k], base[n])
-            slope[n] = jnp.where(above, knot_ref[4 + n, k], slope[n] if k else 0.0)
-    return [base[n] + slope[n] * place for n in range(4)]
+    parts = []
+    for start in range(0, values.shape[0], 8):
+        value = values[start:start + 8]
+        along = value * scale + LIMIT * scale
+        place = jnp.clip(along, 0.0, KNOTS - 1.0)
+        fade = jnp.maximum(1.0 - jnp.abs(along - place), 0.0)
+        index = place.astype(jnp.int32)
+        upper = index >= 8
+        index = index & 7
+        found = [jnp.where(upper, take(high, index), take(low, index)) for low, high in zip(*tables)]
+        parts.append([found[n] + found[4 + n] * place for n in range(4)] + [fade])
+    return [jnp.concatenate(part, axis=0) for part in zip(*parts)]
+
+
+def take(table, index):
+    return jnp.take_along_axis(table, index, axis=0, mode="promise_in_bounds")
 
 
 def render_kernel(flag_ref, color_ref, opacity_ref, volume_ref, front_ref, tail_ref,
-                  pad_ref, table_ref, run_ref, done_ref, seen_ref, knot_ref):
+                  pad_ref, table_ref, run_ref, done_ref):
     step = pl.program_id(0)
     rows_all = front_ref.shape[1]
     groups = rows_all // GROUP
@@ -95,71 +99,53 @@
     @pl.when(step == 0)
     def _():
         build_tables(color_ref, opacity_ref, pad_ref, table_ref)
-        for n in range(8):
-            for k in range(KNOTS + 2):
-                knot_ref[n, k] = pick(table_ref[n, 0:8], jnp.full((8, LANES), k, jnp.int32))
         for ref in (run_ref, done_ref):
             ref[0:3] = jnp.zeros((3, rows_all, LANES), F32)
             ref[3] = jnp.ones((rows_all, LANES), F32)
 
     lane = lane_ids(GROUP)
-    layers = volume_ref.shape[0]
-
-    def look(layer, carry):
-        tables = [table_ref[n, 0:8] for n in range(8)]
-        for start in range(0, rows_all, GROUP):
-            pair = volume_ref[layer, start:start + GROUP, :].astype(F32)
-            for q in range(0, GROUP, 8):
-                at = start + q
-                if at // 8 in CHAINED:
-                    found = climb(pair[q:q + 8], knot_ref)
-                else:
-                    found = classify(pair[q:q + 8], tables)
-                for n in range(4):
-                    seen_ref[n, layer, at:at + 8, :] = found[n]
+    def one(item, carry):
+        tables = read_tables(table_ref)
+        local = item // groups
+        brick = step * bricks + local
+        rows = pl.ds(pl.multiple_of(item % groups * GROUP, GROUP), GROUP)
+        for k in range(BZ):
+            f = k / BZ
+            *shades, alpha, fade = classify(volume_ref[local * BZ + k, rows, :].astype(F32), tables)
+            alpha = alpha * fade
+            if k == 0:
+                weight = alpha * fade
+                here = [weight * shade for shade in shades]
+                clear = 1.0 - alpha
+                continue
+            moved = alpha * f
+            kept = alpha - moved
+            weight = clear * kept * fade
+            beside = pltpu.roll(clear, LANES - 1, 1) * moved * fade
+            here = [h + weight * shade for h, shade in zip(here, shades)]
+            if k == 1:
+                right = [beside * shade for shade in shades]
+            else:
+                right = [r + beside * shade for r, shade in zip(right, shades)]
+            clear = clear - clear * (kept + pltpu.roll(moved, 1, 1))
+        flag = flag_ref[brick].astype(F32)
+        shown = jnp.where(lane == 0, 0.0, flag)
+        passed = jnp.where(lane == LANES - 1, 0.0, flag)
+        image = [pltpu.roll(h * shown, brick, 1) + pltpu.roll(r * passed, brick + 1, 1)
+                 for h, r in zip(here, right)]
+        image.append(pltpu.roll((1.0 - clear) * shown, brick, 1))
+        leaving = lane == brick - 1
+        through = run_ref[3, rows, :]
+        done_ref[3, rows, :] = jnp.where(leaving, through, done_ref[3, rows, :])
+        through = jnp.where(leaving, 1.0, through)
+        for n in range(3):
+            sum_n = run_ref[n, rows, :]
+            done_ref[n, rows, :] = jnp.where(leaving, sum_n, done_ref[n, rows, :])
+            run_ref[n, rows, :] = jnp.where(leaving, 0.0, sum_n) + through * image[n]
+        run_ref[3, rows, :] = through - through * image[3]
         return carry
 
-    lax.fori_loop(0, layers, look, 0, unroll=UNROLL)
-
-    def one(local, carry):
-        brick = step * bricks + local
-        for group in range(groups):
-            rows = slice(group * GROUP, (group + 1) * GROUP)
-            for k in range(BZ):
-                f = k / BZ
-                *shades, alpha = [seen_ref[n, local * BZ + k, rows, :] for n in range(4)]
-                if k == 0:
-                    here = [alpha * shade for shade in shades]
-                    clear = 1.0 - alpha
-                    continue
-                moved = alpha * f
-                kept = alpha - moved
-                weight = clear * kept
-                beside = pltpu.roll(clear, LANES - 1, 1) * moved
-                here = [h + weight * shade for h, shade in zip(here, shades)]
-                if k == 1:
-                    right = [beside * shade for shade in shades]
-                else:
-                    right = [r + beside * shade for r, shade in zip(right, shades)]
-                clear = clear - clear * (kept + pltpu.roll(moved, 1, 1))
-            flag = flag_ref[brick].astype(F32)
-            shown = jnp.where(lane == 0, 0.0, flag)
-            passed = jnp.where(lane == LANES - 1, 0.0, flag)
-            image = [pltpu.roll(h * shown, brick, 1) + pltpu.roll(r * passed, brick + 1, 1)
-                     for h, r in zip(here, right)]
-            image.append(pltpu.roll((1.0 - clear) * shown, brick, 1))
-            leaving = lane == brick - 1
-            through = run_ref[3, rows, :]
-            done_ref[3, rows, :] = jnp.where(leaving, through, done_ref[3, rows, :])
-            through = jnp.where(leaving, 1.0, through)
-            for n in range(3):
-                sum_n = run_ref[n, rows, :]
-                done_ref[n, rows, :] = jnp.where(leaving, sum_n, done_ref[n, rows, :])
-                run_ref[n, rows, :] = jnp.where(leaving, 0.0, sum_n) + through * image[n]
-            run_ref[3, rows, :] = through - through * image[3]
-        return carry
-
-    lax.fori_loop(0, bricks, one, 0)
+    lax.fori_loop(0, bricks * groups, one, 0, unroll=UNROLL)
 
     @pl.when(step == pl.num_programs(0) - 1)
     def _():
@@ -189,11 +175,9 @@
         out_shape=[out, out],
         scratch_shapes=[
             pltpu.VMEM((8, LANES), F32),
-            pltpu.VMEM((8, GROUP, LANES), F32),
+            pltpu.VMEM((2, 8, 8, LANES), F32),
             pltpu.VMEM((4, rows, LANES), F32),
             pltpu.VMEM((4, rows, LANES), F32),
-            pltpu.VMEM((4, layers // STEPS, rows, LANES), F32),
-            pltpu.VMEM((8, KNOTS + 2, 8, LANES), F32),
         ],
         cost_estimate=pl.CostEstimate(flops=40_000_000, bytes_accessed=2_400_000, transcendentals=0),
         compiler_params=pltpu.CompilerParams(vmem_limit_bytes=32 * 1024 * 1024),
@@ -214,11 +198,11 @@
     clear = jnp.ones((bricks, LANES), F32)
     for pair in range(pairs):
         f = jnp.where(second, (2 * pair + 1) / BZ, 2 * pair / BZ)
-        *own, alpha = classify(column_ref[pl.ds(pair, bricks, stride=pairs), :], tables)
-        *left, beside = classify(rim_ref[pl.ds(pair, bricks, stride=pairs), :], tables)
-        kept = (1.0 - f) * alpha
-        moved = f * beside
-        sample = [kept * a + moved * b for a, b in zip(own, left)] + [kept + moved]
+        *own, alpha, fade = classify(column_ref[pl.ds(pair, bricks, stride=pairs), :], tables)
+        *left, beside, side_fade = classify(rim_ref[pl.ds(pair, bricks, stride=pairs), :], tables)
+        kept = (1.0 - f) * (alpha * fade)
+        moved = f * (beside * side_fade)
+        sample = [kept * fade * a + moved * side_fade * b for a, b in zip(own, left)] + [kept + moved]
         for part in (sample, [pltpu.roll(value, rows, 1) for value in sample]):
             image = [total + clear * value for total, value in zip(image, part)]
             clear = clear - clear * part[3]
@@ -228,7 +212,7 @@
 def deal_kernel(layers, flag_ref, color_ref, opacity_ref, column_ref, rim_ref, front_ref, tail_ref, out_ref,
                 pad_ref, table_ref):
     build_tables(color_ref, opacity_ref, pad_ref, table_ref)
-    tables = [table_ref[n] for n in range(8)]
+    tables = read_tables(table_ref)
     step = code_step(opacity_ref[...], layers)
     rows = front_ref.shape[1]
     half = rows // 2
@@ -259,7 +243,7 @@
         out_shape=jax.ShapeDtypeStruct((LANES + GROUP, LANES), jnp.int32),
         scratch_shapes=[
             pltpu.VMEM((8, LANES), F32),
-            pltpu.VMEM((8, GROUP, LANES), F32),
+            pltpu.VMEM((2, 8, 8, LANES), F32),
         ],
         compiler_params=pltpu.CompilerParams(vmem_limit_bytes=32 * 1024 * 1024),
         name="deal",

time: 70.1 us -> 63.5 us (0.906)
  Pallas kernels: 22 us -> 15.4 us
    pallas_call x1, Pallas kernels: 18.7 us -> 12.4 us  [render(): pl.pallas_call(render_kernel, grid=(STEPS,), in_specs=[pl.BlockSpec(memor...]
  transfers between devices with their start and end apart: 1 -> 1, of which waited for: 0 -> 0; matrix products, arithmetic and copies ran while one was open for 0% -> 0% of each run, Pallas kernels for 27% -> 20%
where the time goes in v5:
time: 63.5 us; the launch traced here: 63.3 us
  blocking collectives  42.3 us (67%)
  Pallas kernels  15.4 us (24%)
  starting transfers between devices  3.95 us (6%)
  local copies, waits for them, and re-layouts  1.6 us (3%)
    all_to_all x1, blocking collectives, body(): swapped = lax.all_to_all(rows.reshape(depth, 1, -1), 'gz', 0, 0, tiled=True)  26.4 us
    all_to_all x1, blocking collectives, body(): lax.all_to_all(merged.reshape(across * down, 1, -1), ('gx', 'gy'), 0, 0,...  15.8 us
    pallas_call x1, Pallas kernels, render(): pl.pallas_call(render_kernel, grid=(STEPS,), in_specs=[pl.BlockSpec(memor...  12.4 us
    ppermute x1, starting transfers between devices, body(): rim = lax.ppermute(last, 'gx', [(i, i + 1) for i in range(across - 1)])  3.95 us
    unnamed x8, local copies, waits for them, and re-layouts  1.6 us
  transfers between devices with their start and end apart: 1, of which 0 were waited for; matrix products, arithmetic and copies ran while one was open for 0% of the time, Pallas kernels for 20%

profile of v5, /device:TPU:1, one launch (start us, length us, event | category | flops | bytes accessed | tf_op | source)
XLA Modules:
  0.0 63.3 jit_solution(3341536036443264051)
XLA Ops:
  0.0 0.0 copy-start
  0.0 1.6 %copy-done = bf16[128,64,128]{2,1,0:T(8,128)(2,1)S(1)} copy-done((bf16[128,64,128]{2,1,0:T(8,128)(2,1)S(1)}, bf16[128,64,128]{2,1,0:T(8,128)(2,1)}, u32[]{:S(2)}) %copy-start) | copy-done | bytes 2097176
  1.6 0.0 copy-start.1
  1.6 0.0 copy-start.2
  1.6 0.0 copy-start.3
  1.6 0.6 %ends.1 = (f32[1,8192]{1,0:T(1,128)S(1)}, f32[1,8192]{1,0:T(1,128)S(1)}) custom-call(bf16[128,64,128]{2,1,0:T(8,128)(2,1)S(1)} %copy-done), custom_call_target="tpu_custom_call" | custom-call | tf_op jit(solution)/shard_map/ends/pallas_call | solution.py:340
  2.2 4.0 %collective-permute-start = (f32[64,128]{1,0:T(8,128)S(1)}, f32[64,128]{1,0:T(8,128)S(1)}, u32[]{:S(2)}, u32[]{:S(2)}) collective-permute-start(f32[64,128]{1,0:T(8,128)S(1)} %bitcast.21), channel_id=1, source_target_pairs={{0,128},{128,256},{256,384},{1,129},{129,257},{257,385},{2,130},{1... | collective-permute-start | bytes 98312 | tf_op jit(solution)/shard_map/ppermute | solution.py:356
  6.2 0.0 copy-done.1
  6.2 0.0 copy-done.2
  6.2 0.0 copy-done.3
  6.2 12.4 %render.1 = (f32[4,64,128]{2,1,0:T(8,128)S(1)}, f32[4,64,128]{2,1,0:T(8,128)S(1)}) custom-call(s32[16]{0:T(128)S(1)} %bitcast.19, f32[3,16]{1,0:T(4,128)S(1)} %copy-done.1, f32[1,16]{1,0:T(1,128)S(1)} %bitcast.15, bf16[128,64,128]{2,1,0:T(8,128)(2,1)S(1)} %copy-done), custom_call_target="tpu_custom_call" | custom-call | flops 40000000 | bytes 2400000 | tf_op jit(solution)/shard_map/render/pallas_call | solution.py:165
  18.7 0.0 collective-permute-done.rim_ref
  18.7 1.1 %deal.1 = s32[144,128]{1,0:T(8,128)S(1)} custom-call(s32[16]{0:T(128)S(1)} %bitcast.20, f32[3,16]{1,0:T(4,128)S(1)} %copy-done.1, f32[1,16]{1,0:T(1,128)S(1)} %bitcast.16, f32[64,128]{1,0:T(8,128)S(1)} %bitcast.14, f32[64,128]{1,0:T(8,128)S(1)} %collective-permute-done.rim_ref, f32[4,64,128]{2,1,0:T(8,128)S(1)} %get-tuple-element.11.front_ref, ...), custom_call_target="tpu_custom_call" | custom-call | tf_op jit(solution)/shard_map/deal/pallas_call | solution.py:239
  19.8 26.4 %all_to_all.10 = s32[16,1,1152]{2,1,0:T(1,128)S(1)} all-to-all(s32[16,1,1152]{2,1,0:T(1,128)S(1)} %bitcast.11), channel_id=1, replica_groups=mesh['gx'=4,'gy'=8,'gz'=16] {'gz'}, dimensions={0} | all-to-all | bytes 147456 | tf_op jit(solution)/shard_map/all_to_all | solution.py:359
  46.2 0.3 along_depth.1
  46.5 15.8 %all_to_all.11 = s32[32,1,128]{2,1,0:T(1,128)S(1)} all-to-all(s32[32,1,128]{2,1,0:T(1,128)S(1)} %bitcast.13), channel_id=1, replica_groups=mesh['gx'=4,'gy'=8,'gz'=16] {'gx','gy'}, dimensions={0} | all-to-all | bytes 32768 | tf_op jit(solution)/shard_map/all_to_all | solution.py:361
  62.3 1.0 %gather.1 = f32[4,1,768]{2,1,0:T(1,128)} custom-call(f32[1,16]{1,0:T(1,128)S(1)} %bitcast.18, s32[32,128]{1,0:T(8,128)S(1)} %bitcast.12), custom_call_target="tpu_custom_call" | custom-call | tf_op jit(solution)/shard_map/gather/pallas_call | solution.py:316
Async XLA Ops:
  0.0 1.6 %copy-start = (bf16[128,64,128]{2,1,0:T(8,128)(2,1)S(1)}, bf16[128,64,128]{2,1,0:T(8,128)(2,1)}, u32[]{:S(2)}) copy-start(bf16[128,64,128]{2,1,0:T(8,128)(2,1)} %volume_ref.3) | copy-start | bytes 6291460
  1.6 4.6 %copy-start.1 = (f32[3,16]{1,0:T(4,128)S(1)}, f32[3,16]{1,0:T(4,128)}, u32[]{:S(2)}) copy-start(f32[3,16]{1,0:T(4,128)} %color_ref.3) | copy-start | bytes 580
  1.6 4.6 %copy-start.2 = (f32[16]{0:T(128)S(1)}, f32[16]{0:T(128)}, u32[]{:S(2)}) copy-start(f32[16]{0:T(128)} %param.6) | copy-start | bytes 196
  1.6 4.6 %copy-start.3 = (s32[16,1,1]{0,2,1:T(1,128)S(1)}, s32[16,1,1]{0,2,1:T(1,128)}, u32[]{:S(2)}) copy-start(s32[16,1,1]{0,2,1:T(1,128)} %param.7) | copy-start | bytes 196
  2.2 16.4 %collective-permute-start = (f32[64,128]{1,0:T(8,128)S(1)}, f32[64,128]{1,0:T(8,128)S(1)}, u32[]{:S(2)}, u32[]{:S(2)}) collective-permute-start(f32[64,128]{1,0:T(8,128)S(1)} %bitcast.21), channel_id=1, source_target_pairs={{0,128},{128,256},{256,384},{1,129},{129,257},{257,385},{2,130},{1... | collective-permute-start | bytes 98312 | tf_op jit(solution)/shard_map/ppermute | solution.py:356

commit v6 on v5

--- a/solution.py
+++ b/solution.py
@@ -12,8 +12,6 @@
 KNOTS = 16
 LANES = 128
 GROUP = 16
-STEPS = 4
-UNROLL = 4
 F32 = jnp.float32
 
 
@@ -91,27 +89,22 @@
 
 def render_kernel(flag_ref, color_ref, opacity_ref, volume_ref, front_ref, tail_ref,
                   pad_ref, table_ref, run_ref, done_ref):
-    step = pl.program_id(0)
     rows_all = front_ref.shape[1]
     groups = rows_all // GROUP
     bricks = volume_ref.shape[0] // BZ
 
-    @pl.when(step == 0)
-    def _():
-        build_tables(color_ref, opacity_ref, pad_ref, table_ref)
-        for ref in (run_ref, done_ref):
-            ref[0:3] = jnp.zeros((3, rows_all, LANES), F32)
-            ref[3] = jnp.ones((rows_all, LANES), F32)
+    build_tables(color_ref, opacity_ref, pad_ref, table_ref)
+    for ref in (run_ref, done_ref):
+        ref[0:3] = jnp.zeros((3, rows_all, LANES), F32)
+        ref[3] = jnp.ones((rows_all, LANES), F32)
 
     lane = lane_ids(GROUP)
-    def one(item, carry):
+
+    def group_of(brick, rows):
         tables = read_tables(table_ref)
-        local = item // groups
-        brick = step * bricks + local
-        rows = pl.ds(pl.multiple_of(item % groups * GROUP, GROUP), GROUP)
         for k in range(BZ):
             f = k / BZ
-            *shades, alpha, fade = classify(volume_ref[local * BZ + k, rows, :].astype(F32), tables)
+            *shades, alpha, fade = classify(volume_ref[brick * BZ + k, rows, :].astype(F32), tables)
             alpha = alpha * fade
             if k == 0:
                 weight = alpha * fade
@@ -128,50 +121,50 @@
             else:
                 right = [r + beside * shade for r, shade in zip(right, shades)]
             clear = clear - clear * (kept + pltpu.roll(moved, 1, 1))
-        flag = flag_ref[brick].astype(F32)
-        shown = jnp.where(lane == 0, 0.0, flag)
-        passed = jnp.where(lane == LANES - 1, 0.0, flag)
+        shown = jnp.where(lane == 0, 0.0, 1.0)
+        passed = jnp.where(lane == LANES - 1, 0.0, 1.0)
         image = [pltpu.roll(h * shown, brick, 1) + pltpu.roll(r * passed, brick + 1, 1)
                  for h, r in zip(here, right)]
         image.append(pltpu.roll((1.0 - clear) * shown, brick, 1))
+        through = run_ref[3, rows, :]
+        for n in range(3):
+            run_ref[n, rows, :] = run_ref[n, rows, :] + through * image[n]
+        run_ref[3, rows, :] = through - through * image[3]
+
+    def one(brick, carry):
         leaving = lane == brick - 1
-        through = run_ref[3, rows, :]
-        done_ref[3, rows, :] = jnp.where(leaving, through, done_ref[3, rows, :])
-        through = jnp.where(leaving, 1.0, through)
-        for n in range(3):
-            sum_n = run_ref[n, rows, :]
-            done_ref[n, rows, :] = jnp.where(leaving, sum_n, done_ref[n, rows, :])
-            run_ref[n, rows, :] = jnp.where(leaving, 0.0, sum_n) + through * image[n]
-        run_ref[3, rows, :] = through - through * image[3]
+        for group in range(groups):
+            rows = slice(group * GROUP, (group + 1) * GROUP)
+            for n in range(4):
+                value = run_ref[n, rows, :]
+                done_ref[n, rows, :] = jnp.where(leaving, value, done_ref[n, rows, :])
+                run_ref[n, rows, :] = jnp.where(leaving, float(n == 3), value)
+
+        @pl.when(flag_ref[brick] > 0)
+        def _():
+            for group in range(groups):
+                group_of(brick, slice(group * GROUP, (group + 1) * GROUP))
+
         return carry
 
-    lax.fori_loop(0, bricks * groups, one, 0, unroll=UNROLL)
-
-    @pl.when(step == pl.num_programs(0) - 1)
-    def _():
-        wide = lane_ids(rows_all)
-        total = pl.num_programs(0) * bricks
-        for n in range(4):
-            last = run_ref[n] if n < 3 else 1.0 - run_ref[n]
-            first = done_ref[n] if n < 3 else 1.0 - done_ref[n]
-            front_ref[n] = jnp.where(wide < total - 1, first, last)
-            tail_ref[n] = jnp.where(wide < total - 1, last, 0.0)
+    lax.fori_loop(0, bricks, one, 0)
+
+    wide = lane_ids(rows_all)
+    for n in range(4):
+        last = run_ref[n] if n < 3 else 1.0 - run_ref[n]
+        first = done_ref[n] if n < 3 else 1.0 - done_ref[n]
+        front_ref[n] = jnp.where(wide < bricks - 1, first, last)
+        tail_ref[n] = jnp.where(wide < bricks - 1, last, 0.0)
 
 
 def render(active, tf_color, tf_opacity, volume):
     layers, rows, cols = volume.shape
     out = jax.ShapeDtypeStruct((4, rows, LANES), F32)
-    whole = pl.BlockSpec((4, rows, LANES), lambda i: (0, 0, 0))
+    vmem = pl.BlockSpec(memory_space=pltpu.VMEM)
     return pl.pallas_call(
         render_kernel,
-        grid=(STEPS,),
-        in_specs=[
-            pl.BlockSpec(memory_space=pltpu.SMEM),
-            pl.BlockSpec(tf_color.shape, lambda i: (0, 0)),
-            pl.BlockSpec(tf_opacity.shape, lambda i: (0, 0)),
-            pl.BlockSpec((layers // STEPS, rows, cols), lambda i: (i, 0, 0)),
-        ],
-        out_specs=[whole, whole],
+        in_specs=[pl.BlockSpec(memory_space=pltpu.SMEM), vmem, vmem, vmem],
+        out_specs=[vmem, vmem],
         out_shape=[out, out],
         scratch_shapes=[
             pltpu.VMEM((8, LANES), F32),

time: 63.5 us -> 62.7 us (0.987)
  Pallas kernels: 15.4 us -> 11.2 us
  blocking collectives: 42.3 us -> 45.7 us
    all_to_all x1, blocking collectives: 15.8 us -> 21.3 us  [body(): lax.all_to_all(merged.reshape(across * down, 1, -1), ('gx', 'gy'), 0, 0,...]
    pallas_call x1, Pallas kernels: 12.4 us -> 8.21 us  [render(): pl.pallas_call(render_kernel, in_specs=[pl.BlockSpec(memory_space=pltpu.S...]
    all_to_all x1, blocking collectives: 26.4 us -> 24.4 us  [body(): swapped = lax.all_to_all(rows.reshape(depth, 1, -1), 'gz', 0, 0, tiled=True)]
  transfers between devices with their start and end apart: 1 -> 1, of which waited for: 0 -> 0; matrix products, arithmetic and copies ran while one was open for 0% -> 0% of each run, Pallas kernels for 20% -> 13%
where the time goes in v6:
time: 62.7 us; the launch traced here: 62.5 us
  blocking collectives  45.7 us (73%)
  Pallas kernels  11.2 us (18%)
  starting transfers between devices  3.95 us (6%)
  local copies, waits for them, and re-layouts  1.6 us (3%)
    all_to_all x1, blocking collectives, body(): swapped = lax.all_to_all(rows.reshape(depth, 1, -1), 'gz', 0, 0, tiled=True)  24.4 us
    all_to_all x1, blocking collectives, body(): lax.all_to_all(merged.reshape(across * down, 1, -1), ('gx', 'gy'), 0, 0,...  21.3 us
    pallas_call x1, Pallas kernels, render(): pl.pallas_call(render_kernel, in_specs=[pl.BlockSpec(memory_space=pltpu.S...  8.21 us
    ppermute x1, starting transfers between devices, body(): rim = lax.ppermute(last, 'gx', [(i, i + 1) for i in range(across - 1)])  3.95 us
    unnamed x8, local copies, waits for them, and re-layouts  1.6 us
  transfers between devices with their start and end apart: 1, of which 0 were waited for; matrix products, arithmetic and copies ran while one was open for 0% of the time, Pallas kernels for 13%

profile of v6, /device:TPU:1, one launch (start us, length us, event | category | flops | bytes accessed | tf_op | source)
XLA Modules:
  0.0 62.5 jit_solution(13716406791807466839)
XLA Ops:
  0.0 0.0 copy-start
  0.0 1.6 %copy-done = bf16[128,64,128]{2,1,0:T(8,128)(2,1)S(1)} copy-done((bf16[128,64,128]{2,1,0:T(8,128)(2,1)S(1)}, bf16[128,64,128]{2,1,0:T(8,128)(2,1)}, u32[]{:S(2)}) %copy-start) | copy-done | bytes 2097176
  1.6 0.0 copy-start.1
  1.6 0.0 copy-start.2
  1.6 0.0 copy-start.3
  1.6 0.6 %ends.1 = (f32[1,8192]{1,0:T(1,128)S(1)}, f32[1,8192]{1,0:T(1,128)S(1)}) custom-call(bf16[128,64,128]{2,1,0:T(8,128)(2,1)S(1)} %copy-done), custom_call_target="tpu_custom_call" | custom-call | tf_op jit(solution)/shard_map/ends/pallas_call | solution.py:333
  2.2 4.0 %collective-permute-start = (f32[64,128]{1,0:T(8,128)S(1)}, f32[64,128]{1,0:T(8,128)S(1)}, u32[]{:S(2)}, u32[]{:S(2)}) collective-permute-start(f32[64,128]{1,0:T(8,128)S(1)} %bitcast.21), channel_id=1, source_target_pairs={{0,128},{128,256},{256,384},{1,129},{129,257},{257,385},{2,130},{1... | collective-permute-start | bytes 98312 | tf_op jit(solution)/shard_map/ppermute | solution.py:349
  6.2 0.0 copy-done.1
  6.2 0.0 copy-done.2
  6.2 0.0 copy-done.3
  6.2 8.2 %render.1 = (f32[4,64,128]{2,1,0:T(8,128)S(1)}, f32[4,64,128]{2,1,0:T(8,128)S(1)}) custom-call(s32[16]{0:T(128)S(1)} %bitcast.19, f32[3,16]{1,0:T(4,128)S(1)} %copy-done.1, f32[1,16]{1,0:T(1,128)S(1)} %bitcast.15, bf16[128,64,128]{2,1,0:T(8,128)(2,1)S(1)} %copy-done), custom_call_target="tpu_custom_call" | custom-call | flops 40000000 | bytes 2400000 | tf_op jit(solution)/shard_map/render/pallas_call | solution.py:164
  14.4 0.0 collective-permute-done.rim_ref
  14.5 1.1 %deal.1 = s32[144,128]{1,0:T(8,128)S(1)} custom-call(s32[16]{0:T(128)S(1)} %bitcast.20, f32[3,16]{1,0:T(4,128)S(1)} %copy-done.1, f32[1,16]{1,0:T(1,128)S(1)} %bitcast.16, f32[64,128]{1,0:T(8,128)S(1)} %bitcast.14, f32[64,128]{1,0:T(8,128)S(1)} %collective-permute-done.rim_ref, f32[4,64,128]{2,1,0:T(8,128)S(1)} %get-tuple-element.11.front_ref, ...), custom_call_target="tpu_custom_call" | custom-call | tf_op jit(solution)/shard_map/deal/pallas_call | solution.py:232
  15.6 24.4 %all_to_all.10 = s32[16,1,1152]{2,1,0:T(1,128)S(1)} all-to-all(s32[16,1,1152]{2,1,0:T(1,128)S(1)} %bitcast.11), channel_id=1, replica_groups=mesh['gx'=4,'gy'=8,'gz'=16] {'gz'}, dimensions={0} | all-to-all | bytes 147456 | tf_op jit(solution)/shard_map/all_to_all | solution.py:352
  39.9 0.3 along_depth.1
  40.3 21.3 %all_to_all.11 = s32[32,1,128]{2,1,0:T(1,128)S(1)} all-to-all(s32[32,1,128]{2,1,0:T(1,128)S(1)} %bitcast.13), channel_id=1, replica_groups=mesh['gx'=4,'gy'=8,'gz'=16] {'gx','gy'}, dimensions={0} | all-to-all | bytes 32768 | tf_op jit(solution)/shard_map/all_to_all | solution.py:354
  61.6 1.0 %gather.1 = f32[4,1,768]{2,1,0:T(1,128)} custom-call(f32[1,16]{1,0:T(1,128)S(1)} %bitcast.18, s32[32,128]{1,0:T(8,128)S(1)} %bitcast.12), custom_call_target="tpu_custom_call" | custom-call | tf_op jit(solution)/shard_map/gather/pallas_call | solution.py:309
Async XLA Ops:
  0.0 1.6 %copy-start = (bf16[128,64,128]{2,1,0:T(8,128)(2,1)S(1)}, bf16[128,64,128]{2,1,0:T(8,128)(2,1)}, u32[]{:S(2)}) copy-start(bf16[128,64,128]{2,1,0:T(8,128)(2,1)} %volume_ref.3) | copy-start | bytes 6291460
  1.6 4.6 %copy-start.1 = (f32[3,16]{1,0:T(4,128)S(1)}, f32[3,16]{1,0:T(4,128)}, u32[]{:S(2)}) copy-start(f32[3,16]{1,0:T(4,128)} %color_ref.3) | copy-start | bytes 580
  1.6 4.6 %copy-start.2 = (f32[16]{0:T(128)S(1)}, f32[16]{0:T(128)}, u32[]{:S(2)}) copy-start(f32[16]{0:T(128)} %param.6) | copy-start | bytes 196
  1.6 4.6 %copy-start.3 = (s32[16,1,1]{0,2,1:T(1,128)S(1)}, s32[16,1,1]{0,2,1:T(1,128)}, u32[]{:S(2)}) copy-start(s32[16,1,1]{0,2,1:T(1,128)} %param.7) | copy-start | bytes 196
  2.2 12.2 %collective-permute-start = (f32[64,128]{1,0:T(8,128)S(1)}, f32[64,128]{1,0:T(8,128)S(1)}, u32[]{:S(2)}, u32[]{:S(2)}) collective-permute-start(f32[64,128]{1,0:T(8,128)S(1)} %bitcast.21), channel_id=1, source_target_pairs={{0,128},{128,256},{256,384},{1,129},{129,257},{257,385},{2,130},{1... | collective-permute-start | bytes 98312 | tf_op jit(solution)/shard_map/ppermute | solution.py:349

commit v7 on v6

--- a/solution.py
+++ b/solution.py
@@ -87,9 +87,8 @@
     return jnp.take_along_axis(table, index, axis=0, mode="promise_in_bounds")
 
 
-def render_kernel(flag_ref, color_ref, opacity_ref, volume_ref, front_ref, tail_ref,
-                  pad_ref, table_ref, run_ref, done_ref):
-    rows_all = front_ref.shape[1]
+def render_kernel(flag_ref, color_ref, opacity_ref, volume_ref, run_ref, done_ref, table_ref, pad_ref):
+    rows_all = run_ref.shape[1]
     groups = rows_all // GROUP
     bricks = volume_ref.shape[0] // BZ
 
@@ -131,8 +130,8 @@
             run_ref[n, rows, :] = run_ref[n, rows, :] + through * image[n]
         run_ref[3, rows, :] = through - through * image[3]
 
-    def one(brick, carry):
-        leaving = lane == brick - 1
+    def leave(first, last):
+        leaving = (lane >= first) & (lane < last)
         for group in range(groups):
             rows = slice(group * GROUP, (group + 1) * GROUP)
             for n in range(4):
@@ -140,42 +139,34 @@
                 done_ref[n, rows, :] = jnp.where(leaving, value, done_ref[n, rows, :])
                 run_ref[n, rows, :] = jnp.where(leaving, float(n == 3), value)
 
-        @pl.when(flag_ref[brick] > 0)
+    def one(brick, left):
+        active = flag_ref[brick] > 0
+
+        @pl.when(active)
         def _():
+            leave(left, brick)
             for group in range(groups):
                 group_of(brick, slice(group * GROUP, (group + 1) * GROUP))
 
-        return carry
-
-    lax.fori_loop(0, bricks, one, 0)
-
-    wide = lane_ids(rows_all)
-    for n in range(4):
-        last = run_ref[n] if n < 3 else 1.0 - run_ref[n]
-        first = done_ref[n] if n < 3 else 1.0 - done_ref[n]
-        front_ref[n] = jnp.where(wide < bricks - 1, first, last)
-        tail_ref[n] = jnp.where(wide < bricks - 1, last, 0.0)
-
-
-def render(active, tf_color, tf_opacity, volume):
-    layers, rows, cols = volume.shape
+        return jnp.where(active, brick, left)
+
+    leave(lax.fori_loop(0, bricks, one, 0), bricks - 1)
+
+
+def render(flags, tf_color, tf_opacity, volume):
+    rows = volume.shape[1]
     out = jax.ShapeDtypeStruct((4, rows, LANES), F32)
     vmem = pl.BlockSpec(memory_space=pltpu.VMEM)
     return pl.pallas_call(
         render_kernel,
         in_specs=[pl.BlockSpec(memory_space=pltpu.SMEM), vmem, vmem, vmem],
-        out_specs=[vmem, vmem],
-        out_shape=[out, out],
-        scratch_shapes=[
-            pltpu.VMEM((8, LANES), F32),
-            pltpu.VMEM((2, 8, 8, LANES), F32),
-            pltpu.VMEM((4, rows, LANES), F32),
-            pltpu.VMEM((4, rows, LANES), F32),
-        ],
+        out_specs=[vmem, vmem, vmem],
+        out_shape=[out, out, jax.ShapeDtypeStruct((2, 8, 8, LANES), F32)],
+        scratch_shapes=[pltpu.VMEM((8, LANES), F32)],
         cost_estimate=pl.CostEstimate(flops=40_000_000, bytes_accessed=2_400_000, transcendentals=0),
         compiler_params=pltpu.CompilerParams(vmem_limit_bytes=32 * 1024 * 1024),
         name="render",
-    )(active, tf_color, tf_opacity, volume)
+    )(flags, tf_color, tf_opacity, volume)
 
 
 def rim_image(column_ref, rim_ref, flag_ref, tables, rows):
@@ -202,24 +193,26 @@
     return [value * flags for value in image]
 
 
-def deal_kernel(layers, flag_ref, color_ref, opacity_ref, column_ref, rim_ref, front_ref, tail_ref, out_ref,
-                pad_ref, table_ref):
-    build_tables(color_ref, opacity_ref, pad_ref, table_ref)
+def deal_kernel(layers, flag_ref, table_ref, opacity_ref, column_ref, rim_ref, run_ref, done_ref, out_ref):
     tables = read_tables(table_ref)
     step = code_step(opacity_ref[...], layers)
-    rows = front_ref.shape[1]
+    rows = run_ref.shape[1]
     half = rows // 2
     lane = lane_ids(GROUP)
     to_alpha = lane % half + 3 * half
     rim = rim_image(column_ref, rim_ref, flag_ref, tables, rows)
     pieces = LANES // GROUP + 1
     near, far, image = [], [], []
+    begun = lane_ids(half) < layers // BZ - 1
     for parity in range(2):
         spread = [pick(value, lane % half * 2 + parity) for value in rim]
         image.append(jnp.where(lane < half, spread[0], jnp.where(
             lane < 2 * half, spread[1], jnp.where(lane < 3 * half, spread[2], spread[3]))))
-        near.append(jnp.concatenate([front_ref[n, pl.ds(parity, half, stride=2), :] for n in range(4)], axis=0).T)
-        far.append(jnp.concatenate([tail_ref[n, pl.ds(parity, half, stride=2), :] for n in range(4)], axis=0).T)
+        place = pl.ds(parity, half, stride=2)
+        run = [run_ref[n, place, :] for n in range(3)] + [1.0 - run_ref[3, place, :]]
+        done = [done_ref[n, place, :] for n in range(3)] + [1.0 - done_ref[3, place, :]]
+        near.append(jnp.concatenate([jnp.where(begun, d, r) for d, r in zip(done, run)], axis=0).T)
+        far.append(jnp.concatenate([jnp.where(begun, r, 0.0) for r in run], axis=0).T)
     for m in range(pieces):
         pair = [n[m * GROUP:(m + 1) * GROUP] if m < pieces - 1 else f[:GROUP] for n, f in zip(near, far)]
         if m == 0:
@@ -227,20 +220,16 @@
         out_ref[pl.ds(m, GROUP, stride=pieces), :] = pack(*pair, step)
 
 
-def deal(layers, flags, tf_color, tf_opacity, column, rim, front, tail):
+def deal(layers, flags, tables, tf_opacity, column, rim, running, finished):
     vmem = pl.BlockSpec(memory_space=pltpu.VMEM)
     return pl.pallas_call(
         functools.partial(deal_kernel, layers),
         in_specs=[pl.BlockSpec(memory_space=pltpu.SMEM)] + [vmem] * 6,
         out_specs=vmem,
         out_shape=jax.ShapeDtypeStruct((LANES + GROUP, LANES), jnp.int32),
-        scratch_shapes=[
-            pltpu.VMEM((8, LANES), F32),
-            pltpu.VMEM((2, 8, 8, LANES), F32),
-        ],
         compiler_params=pltpu.CompilerParams(vmem_limit_bytes=32 * 1024 * 1024),
         name="deal",
-    )(flags, tf_color, tf_opacity, column, rim, front, tail)
+    )(flags, tables, tf_opacity, column, rim, running, finished)
 
 
 def along_depth_kernel(across, down, depth, layers, opacity_ref, arrived_ref, out_ref, total_ref, clear_ref):
@@ -347,8 +336,8 @@
     flags = active.reshape(bricks)
     column, last = ends(volume)
     rim = lax.ppermute(last, "gx", [(i, i + 1) for i in range(across - 1)])
-    front, tail = render(flags, tf_color, opacity, volume)
-    rows = deal(layers, flags, tf_color, opacity, column, rim, front, tail)
+    running, finished, tables = render(flags, tf_color, opacity, volume)
+    rows = deal(layers, flags, tables, opacity, column, rim, running, finished)
     swapped = lax.all_to_all(rows.reshape(depth, 1, -1), "gz", 0, 0, tiled=True)
     merged = along_depth(layers, opacity, swapped.reshape(-1, LANES), across, down, depth)
     arrived = lax.all_to_all(merged.reshape(across * down, 1, -1), ("gx", "gy"), 0, 0, tiled=True)

time: 62.7 us -> 59.4 us (0.947)
  Pallas kernels: 11.2 us -> 9.49 us
  blocking collectives: 45.7 us -> 44.4 us
    all_to_all x1, blocking collectives: 21.3 us -> 17.2 us  [body(): lax.all_to_all(merged.reshape(across * down, 1, -1), ('gx', 'gy'), 0, 0,...]
    all_to_all x1, blocking collectives: 24.4 us -> 27.1 us  [body(): swapped = lax.all_to_all(rows.reshape(depth, 1, -1), 'gz', 0, 0, tiled=True)]
    pallas_call x1, Pallas kernels: 8.21 us -> 6.58 us  [render(): pl.pallas_call(render_kernel, in_specs=[pl.BlockSpec(memory_space=pltpu.S...]
    unnamed x8 -> x10, local copies, waits for them, and re-layouts: 1.6 us -> 1.61 us
  transfers between devices with their start and end apart: 1 -> 1, of which waited for: 0 -> 0; matrix products, arithmetic and copies ran while one was open for 0% -> 0% of each run, Pallas kernels for 13% -> 11%
where the time goes in v7:
time: 59.4 us; the launch traced here: 59.5 us
  blocking collectives  44.4 us (75%)
  Pallas kernels  9.49 us (16%)
  starting transfers between devices  3.95 us (7%)
  local copies, waits for them, and re-layouts  1.61 us (3%)
    all_to_all x1, blocking collectives, body(): swapped = lax.all_to_all(rows.reshape(depth, 1, -1), 'gz', 0, 0, tiled=True)  27.1 us
    all_to_all x1, blocking collectives, body(): lax.all_to_all(merged.reshape(across * down, 1, -1), ('gx', 'gy'), 0, 0,...  17.2 us
    pallas_call x1, Pallas kernels, render(): pl.pallas_call(render_kernel, in_specs=[pl.BlockSpec(memory_space=pltpu.S...  6.58 us
    ppermute x1, starting transfers between devices, body(): rim = lax.ppermute(last, 'gx', [(i, i + 1) for i in range(across - 1)])  3.95 us
    unnamed x10, local copies, waits for them, and re-layouts  1.61 us
  transfers between devices with their start and end apart: 1, of which 0 were waited for; matrix products, arithmetic and copies ran while one was open for 0% of the time, Pallas kernels for 11%

profile of v7, /device:TPU:1, one launch (start us, length us, event | category | flops | bytes accessed | tf_op | source)
XLA Modules:
  0.0 59.5 jit_solution(10337976756433089393)
XLA Ops:
  0.0 0.0 copy-start
  0.0 1.6 %copy-done = bf16[128,64,128]{2,1,0:T(8,128)(2,1)S(1)} copy-done((bf16[128,64,128]{2,1,0:T(8,128)(2,1)S(1)}, bf16[128,64,128]{2,1,0:T(8,128)(2,1)}, u32[]{:S(2)}) %copy-start) | copy-done | bytes 2097176
  1.6 0.0 copy-start.1
  1.6 0.0 copy-start.2
  1.6 0.0 copy-start.3
  1.6 0.0 copy-start.4
  1.6 0.6 %ends.1 = (f32[1,8192]{1,0:T(1,128)S(1)}, f32[1,8192]{1,0:T(1,128)S(1)}) custom-call(bf16[128,64,128]{2,1,0:T(8,128)(2,1)S(1)} %copy-done), custom_call_target="tpu_custom_call" | custom-call | tf_op jit(solution)/shard_map/ends/pallas_call | solution.py:322
  2.3 4.0 %collective-permute-start = (f32[64,128]{1,0:T(8,128)S(1)}, f32[64,128]{1,0:T(8,128)S(1)}, u32[]{:S(2)}, u32[]{:S(2)}) collective-permute-start(f32[64,128]{1,0:T(8,128)S(1)} %bitcast.21), channel_id=1, source_target_pairs={{0,128},{128,256},{256,384},{1,129},{129,257},{257,385},{2,130},{1... | collective-permute-start | bytes 98312 | tf_op jit(solution)/shard_map/ppermute | solution.py:338
  6.2 0.0 copy-done.1
  6.2 0.0 copy-done.2
  6.2 0.0 copy-done.3
  6.2 0.0 copy-done.4
  6.3 6.6 %render.1 = (f32[4,64,128]{2,1,0:T(8,128)S(1)}, f32[4,64,128]{2,1,0:T(8,128)S(1)}, f32[2,8,8,128]{3,2,1,0:T(8,128)S(1)}) custom-call(s32[16]{0:T(128)S(1)} %bitcast.19, f32[3,16]{1,0:T(4,128)S(1)} %copy-done.3, f32[1,16]{1,0:T(1,128)S(1)} %bitcast.15, bf16[128,64,128]{2,1,0:T(8,128)(2,1)S(1)} %copy-done.1), custom_call_target="tpu_custom_call" | custom-call | flops 40000000 | bytes 2400000 | tf_op jit(solution)/shard_map/render/pallas_call | solution.py:160
  12.8 0.0 collective-permute-done.rim_ref
  12.9 1.0 %deal.1 = s32[144,128]{1,0:T(8,128)S(1)} custom-call(s32[16]{0:T(128)S(1)} %bitcast.20, f32[2,8,8,128]{3,2,1,0:T(8,128)S(1)} %get-tuple-element.10.table_ref, f32[1,16]{1,0:T(1,128)S(1)} %bitcast.16, f32[64,128]{1,0:T(8,128)S(1)} %bitcast.14, f32[64,128]{1,0:T(8,128)S(1)} %collective-permute-done.rim_ref, f32[4,64,128]{2,1,0:T(8,128)S(1)} %get-tuple-element.13.run_ref, ...), custom_call_target="tpu_custom_call" | custom-call | tf_op jit(solution)/shard_map/deal/pallas_call | solution.py:225
  13.9 27.1 %all_to_all.10 = s32[16,1,1152]{2,1,0:T(1,128)S(1)} all-to-all(s32[16,1,1152]{2,1,0:T(1,128)S(1)} %bitcast.10), channel_id=1, replica_groups=mesh['gx'=4,'gy'=8,'gz'=16] {'gz'}, dimensions={0} | all-to-all | bytes 147456 | tf_op jit(solution)/shard_map/all_to_all | solution.py:341
  41.0 0.3 along_depth.1
  41.3 17.2 %all_to_all.11 = s32[32,1,128]{2,1,0:T(1,128)S(1)} all-to-all(s32[32,1,128]{2,1,0:T(1,128)S(1)} %bitcast.13), channel_id=1, replica_groups=mesh['gx'=4,'gy'=8,'gz'=16] {'gx','gy'}, dimensions={0} | all-to-all | bytes 32768 | tf_op jit(solution)/shard_map/all_to_all | solution.py:343
  58.5 1.0 %gather.1 = f32[4,1,768]{2,1,0:T(1,128)} custom-call(f32[1,16]{1,0:T(1,128)S(1)} %bitcast.18, s32[32,128]{1,0:T(8,128)S(1)} %bitcast.12), custom_call_target="tpu_custom_call" | custom-call | tf_op jit(solution)/shard_map/gather/pallas_call | solution.py:298
Async XLA Ops:
  0.0 1.6 %copy-start = (bf16[128,64,128]{2,1,0:T(8,128)(2,1)S(1)}, bf16[128,64,128]{2,1,0:T(8,128)(2,1)}, u32[]{:S(2)}) copy-start(bf16[128,64,128]{2,1,0:T(8,128)(2,1)} %volume_ref.3) | copy-start | bytes 6291460
  1.6 4.6 %copy-start.1 = (bf16[128,64,128]{2,1,0:T(8,128)(2,1)S(1)}, bf16[128,64,128]{2,1,0:T(8,128)(2,1)}, u32[]{:S(2)}) copy-start(bf16[128,64,128]{2,1,0:T(8,128)(2,1)} %volume_ref.3) | copy-start | bytes 6291460
  1.6 4.6 %copy-start.2 = (f32[16]{0:T(128)S(1)}, f32[16]{0:T(128)}, u32[]{:S(2)}) copy-start(f32[16]{0:T(128)} %param.6) | copy-start | bytes 196
  1.6 4.6 %copy-start.3 = (f32[3,16]{1,0:T(4,128)S(1)}, f32[3,16]{1,0:T(4,128)}, u32[]{:S(2)}) copy-start(f32[3,16]{1,0:T(4,128)} %color_ref.1) | copy-start | bytes 580
  1.6 4.6 %copy-start.4 = (s32[16,1,1]{0,2,1:T(1,128)S(1)}, s32[16,1,1]{0,2,1:T(1,128)}, u32[]{:S(2)}) copy-start(s32[16,1,1]{0,2,1:T(1,128)} %param.7) | copy-start | bytes 196
  2.3 10.6 %collective-permute-start = (f32[64,128]{1,0:T(8,128)S(1)}, f32[64,128]{1,0:T(8,128)S(1)}, u32[]{:S(2)}, u32[]{:S(2)}) collective-permute-start(f32[64,128]{1,0:T(8,128)S(1)} %bitcast.21), channel_id=1, source_target_pairs={{0,128},{128,256},{256,384},{1,129},{129,257},{257,385},{2,130},{1... | collective-permute-start | bytes 98312 | tf_op jit(solution)/shard_map/ppermute | solution.py:338

commit v8 on v7

--- a/solution.py
+++ b/solution.py
@@ -12,6 +12,7 @@
 KNOTS = 16
 LANES = 128
 GROUP = 16
+STRIP = 32
 F32 = jnp.float32
 
 
@@ -53,33 +54,30 @@
     pad_ref[3:4, 0:KNOTS] = opacity_ref[...]
     knots = pad_ref[...]
     lane = lane_ids(8)
-    slope = jnp.where(lane < KNOTS - 1, pltpu.roll(knots, LANES - 1, 1) - knots, 0.0)
-    base = knots - slope * lane.astype(F32)
+    rise = pltpu.roll(knots, LANES - 1, 1) - knots
+    bend = jnp.where(lane < KNOTS - 2, pltpu.roll(rise, LANES - 1, 1) - rise, 0.0)
     row = lax.broadcasted_iota(jnp.int32, (8, LANES), 0)
-    for half in range(2):
+    for m, source in enumerate((2.0 * knots, 4.0 * rise, 4.0 * bend)):
         for n in range(4):
-            for m, source in enumerate((base, slope)):
-                spread = jnp.broadcast_to(source[n:n + 1], (8, LANES))
-                table_ref[half, m * 4 + n] = pick(spread, row + 8 * half)
+            table_ref[m * 4 + n] = pick(jnp.broadcast_to(source[n:n + 1], (8, LANES)), 2 * row)
 
 
 def read_tables(table_ref):
-    return [[table_ref[half, n] for n in range(8)] for half in range(2)]
+    return [table_ref[n] for n in range(12)]
 
 
 def classify(values, tables):
-    scale = (KNOTS - 1) / (2.0 * LIMIT)
+    scale = 0.5 * (KNOTS - 1) / (2.0 * LIMIT)
     parts = []
     for start in range(0, values.shape[0], 8):
-        value = values[start:start + 8]
-        along = value * scale + LIMIT * scale
-        place = jnp.clip(along, 0.0, KNOTS - 1.0)
-        fade = jnp.maximum(1.0 - jnp.abs(along - place), 0.0)
+        along = values[start:start + 8] * scale + LIMIT * scale
+        place = jnp.clip(along, 0.0, 0.5 * (KNOTS - 1))
+        fade = jnp.maximum(0.5 - jnp.abs(along - place), 0.0)
         index = place.astype(jnp.int32)
-        upper = index >= 8
-        index = index & 7
-        found = [jnp.where(upper, take(high, index), take(low, index)) for low, high in zip(*tables)]
-        parts.append([found[n] + found[4 + n] * place for n in range(4)] + [fade])
+        place = place - index.astype(F32)
+        past = jnp.maximum(place - 0.5, 0.0)
+        base, slope, bend = [[take(table, index) for table in tables[m:m + 4]] for m in (0, 4, 8)]
+        parts.append([base[n] + slope[n] * place + bend[n] * past for n in range(4)] + [fade])
     return [jnp.concatenate(part, axis=0) for part in zip(*parts)]
 
 
@@ -89,7 +87,7 @@
 
 def render_kernel(flag_ref, color_ref, opacity_ref, volume_ref, run_ref, done_ref, table_ref, pad_ref):
     rows_all = run_ref.shape[1]
-    groups = rows_all // GROUP
+    groups = rows_all // STRIP
     bricks = volume_ref.shape[0] // BZ
 
     build_tables(color_ref, opacity_ref, pad_ref, table_ref)
@@ -97,7 +95,7 @@
         ref[0:3] = jnp.zeros((3, rows_all, LANES), F32)
         ref[3] = jnp.ones((rows_all, LANES), F32)
 
-    lane = lane_ids(GROUP)
+    lane = lane_ids(STRIP)
 
     def group_of(brick, rows):
         tables = read_tables(table_ref)
@@ -133,7 +131,7 @@
     def leave(first, last):
         leaving = (lane >= first) & (lane < last)
         for group in range(groups):
-            rows = slice(group * GROUP, (group + 1) * GROUP)
+            rows = slice(group * STRIP, (group + 1) * STRIP)
             for n in range(4):
                 value = run_ref[n, rows, :]
                 done_ref[n, rows, :] = jnp.where(leaving, value, done_ref[n, rows, :])
@@ -146,7 +144,7 @@
         def _():
             leave(left, brick)
             for group in range(groups):
-                group_of(brick, slice(group * GROUP, (group + 1) * GROUP))
+                group_of(brick, slice(group * STRIP, (group + 1) * STRIP))
 
         return jnp.where(active, brick, left)
 
@@ -161,7 +159,7 @@
         render_kernel,
         in_specs=[pl.BlockSpec(memory_space=pltpu.SMEM), vmem, vmem, vmem],
         out_specs=[vmem, vmem, vmem],
-        out_shape=[out, out, jax.ShapeDtypeStruct((2, 8, 8, LANES), F32)],
+        out_shape=[out, out, jax.ShapeDtypeStruct((12, 8, LANES), F32)],
         scratch_shapes=[pltpu.VMEM((8, LANES), F32)],
         cost_estimate=pl.CostEstimate(flops=40_000_000, bytes_accessed=2_400_000, transcendentals=0),
         compiler_params=pltpu.CompilerParams(vmem_limit_bytes=32 * 1024 * 1024),

time: 59.4 us -> 59.8 us (level)
  blocking collectives: 44.4 us -> 46 us
  Pallas kernels: 9.49 us -> 7.95 us
    all_to_all x1, blocking collectives: 27.1 us -> 30.5 us  [body(): swapped = lax.all_to_all(rows.reshape(depth, 1, -1), 'gz', 0, 0, tiled=True)]
    all_to_all x1, blocking collectives: 17.2 us -> 15.5 us  [body(): lax.all_to_all(merged.reshape(across * down, 1, -1), ('gx', 'gy'), 0, 0,...]
    pallas_call x1, Pallas kernels: 6.58 us -> 5.05 us  [render(): pl.pallas_call(render_kernel, in_specs=[pl.BlockSpec(memory_space=pltpu.S...]
  transfers between devices with their start and end apart: 1 -> 1, of which waited for: 0 -> 0; matrix products, arithmetic and copies ran while one was open for 0% -> 0% of each run, Pallas kernels for 11% -> 8%
where the time goes in v8:
time: 59.8 us; the launch traced here: 59.6 us
  blocking collectives  46 us (77%)
  Pallas kernels  7.95 us (13%)
  starting transfers between devices  3.95 us (7%)
  local copies, waits for them, and re-layouts  1.61 us (3%)
    all_to_all x1, blocking collectives, body(): swapped = lax.all_to_all(rows.reshape(depth, 1, -1), 'gz', 0, 0, tiled=True)  30.5 us
    all_to_all x1, blocking collectives, body(): lax.all_to_all(merged.reshape(across * down, 1, -1), ('gx', 'gy'), 0, 0,...  15.5 us
    pallas_call x1, Pallas kernels, render(): pl.pallas_call(render_kernel, in_specs=[pl.BlockSpec(memory_space=pltpu.S...  5.05 us
    ppermute x1, starting transfers between devices, body(): rim = lax.ppermute(last, 'gx', [(i, i + 1) for i in range(across - 1)])  3.95 us
    unnamed x10, local copies, waits for them, and re-layouts  1.61 us
  transfers between devices with their start and end apart: 1, of which 0 were waited for; matrix products, arithmetic and copies ran while one was open for 0% of the time, Pallas kernels for 8%

profile of v8, /device:TPU:1, one launch (start us, length us, event | category | flops | bytes accessed | tf_op | source)
XLA Modules:
  0.0 59.6 jit_solution(4478530448098593671)
XLA Ops:
  0.0 0.0 copy-start
  0.0 1.6 %copy-done = bf16[128,64,128]{2,1,0:T(8,128)(2,1)S(1)} copy-done((bf16[128,64,128]{2,1,0:T(8,128)(2,1)S(1)}, bf16[128,64,128]{2,1,0:T(8,128)(2,1)}, u32[]{:S(2)}) %copy-start) | copy-done | bytes 2097176
  1.6 0.0 copy-start.1
  1.6 0.0 copy-start.2
  1.6 0.0 copy-start.3
  1.6 0.0 copy-start.4
  1.6 0.6 %ends.1 = (f32[1,8192]{1,0:T(1,128)S(1)}, f32[1,8192]{1,0:T(1,128)S(1)}) custom-call(bf16[128,64,128]{2,1,0:T(8,128)(2,1)S(1)} %copy-done), custom_call_target="tpu_custom_call" | custom-call | tf_op jit(solution)/shard_map/ends/pallas_call | solution.py:320
  2.3 4.0 %collective-permute-start = (f32[64,128]{1,0:T(8,128)S(1)}, f32[64,128]{1,0:T(8,128)S(1)}, u32[]{:S(2)}, u32[]{:S(2)}) collective-permute-start(f32[64,128]{1,0:T(8,128)S(1)} %bitcast.21), channel_id=1, source_target_pairs={{0,128},{128,256},{256,384},{1,129},{129,257},{257,385},{2,130},{1... | collective-permute-start | bytes 98312 | tf_op jit(solution)/shard_map/ppermute | solution.py:336
  6.2 0.0 copy-done.1
  6.2 0.0 copy-done.2
  6.2 0.0 copy-done.3
  6.2 0.0 copy-done.4
  6.3 5.0 %render.1 = (f32[4,64,128]{2,1,0:T(8,128)S(1)}, f32[4,64,128]{2,1,0:T(8,128)S(1)}, f32[12,8,128]{2,1,0:T(8,128)S(1)}) custom-call(s32[16]{0:T(128)S(1)} %bitcast.19, f32[3,16]{1,0:T(4,128)S(1)} %copy-done.3, f32[1,16]{1,0:T(1,128)S(1)} %bitcast.15, bf16[128,64,128]{2,1,0:T(8,128)(2,1)S(1)} %copy-done.1), custom_call_target="tpu_custom_call" | custom-call | flops 40000000 | bytes 2400000 | tf_op jit(solution)/shard_map/render/pallas_call | solution.py:158
  11.3 0.0 collective-permute-done.rim_ref
  11.3 1.0 %deal.1 = s32[144,128]{1,0:T(8,128)S(1)} custom-call(s32[16]{0:T(128)S(1)} %bitcast.20, f32[12,8,128]{2,1,0:T(8,128)S(1)} %get-tuple-element.10.table_ref, f32[1,16]{1,0:T(1,128)S(1)} %bitcast.16, f32[64,128]{1,0:T(8,128)S(1)} %bitcast.14, f32[64,128]{1,0:T(8,128)S(1)} %collective-permute-done.rim_ref, f32[4,64,128]{2,1,0:T(8,128)S(1)} %get-tuple-element.13.run_ref, ...), custom_call_target="tpu_custom_call" | custom-call | tf_op jit(solution)/shard_map/deal/pallas_call | solution.py:223
  12.3 30.5 %all_to_all.10 = s32[16,1,1152]{2,1,0:T(1,128)S(1)} all-to-all(s32[16,1,1152]{2,1,0:T(1,128)S(1)} %bitcast.10), channel_id=1, replica_groups=mesh['gx'=4,'gy'=8,'gz'=16] {'gz'}, dimensions={0} | all-to-all | bytes 147456 | tf_op jit(solution)/shard_map/all_to_all | solution.py:339
  42.9 0.3 along_depth.1
  43.2 15.5 %all_to_all.11 = s32[32,1,128]{2,1,0:T(1,128)S(1)} all-to-all(s32[32,1,128]{2,1,0:T(1,128)S(1)} %bitcast.13), channel_id=1, replica_groups=mesh['gx'=4,'gy'=8,'gz'=16] {'gx','gy'}, dimensions={0} | all-to-all | bytes 32768 | tf_op jit(solution)/shard_map/all_to_all | solution.py:341
  58.6 1.0 %gather.1 = f32[4,1,768]{2,1,0:T(1,128)} custom-call(f32[1,16]{1,0:T(1,128)S(1)} %bitcast.18, s32[32,128]{1,0:T(8,128)S(1)} %bitcast.12), custom_call_target="tpu_custom_call" | custom-call | tf_op jit(solution)/shard_map/gather/pallas_call | solution.py:296
Async XLA Ops:
  0.0 1.6 %copy-start = (bf16[128,64,128]{2,1,0:T(8,128)(2,1)S(1)}, bf16[128,64,128]{2,1,0:T(8,128)(2,1)}, u32[]{:S(2)}) copy-start(bf16[128,64,128]{2,1,0:T(8,128)(2,1)} %volume_ref.3) | copy-start | bytes 6291460
  1.6 4.6 %copy-start.1 = (bf16[128,64,128]{2,1,0:T(8,128)(2,1)S(1)}, bf16[128,64,128]{2,1,0:T(8,128)(2,1)}, u32[]{:S(2)}) copy-start(bf16[128,64,128]{2,1,0:T(8,128)(2,1)} %volume_ref.3) | copy-start | bytes 6291460
  1.6 4.6 %copy-start.2 = (f32[16]{0:T(128)S(1)}, f32[16]{0:T(128)}, u32[]{:S(2)}) copy-start(f32[16]{0:T(128)} %param.6) | copy-start | bytes 196
  1.6 4.6 %copy-start.3 = (f32[3,16]{1,0:T(4,128)S(1)}, f32[3,16]{1,0:T(4,128)}, u32[]{:S(2)}) copy-start(f32[3,16]{1,0:T(4,128)} %color_ref.1) | copy-start | bytes 580
  1.6 4.6 %copy-start.4 = (s32[16,1,1]{0,2,1:T(1,128)S(1)}, s32[16,1,1]{0,2,1:T(1,128)}, u32[]{:S(2)}) copy-start(s32[16,1,1]{0,2,1:T(1,128)} %param.7) | copy-start | bytes 196
  2.3 9.1 %collective-permute-start = (f32[64,128]{1,0:T(8,128)S(1)}, f32[64,128]{1,0:T(8,128)S(1)}, u32[]{:S(2)}, u32[]{:S(2)}) collective-permute-start(f32[64,128]{1,0:T(8,128)S(1)} %bitcast.21), channel_id=1, source_target_pairs={{0,128},{128,256},{256,384},{1,129},{129,257},{257,385},{2,130},{1... | collective-permute-start | bytes 98312 | tf_op jit(solution)/shard_map/ppermute | solution.py:336

commit v9 on v8

--- a/solution.py
+++ b/solution.py
@@ -118,15 +118,12 @@
             else:
                 right = [r + beside * shade for r, shade in zip(right, shades)]
             clear = clear - clear * (kept + pltpu.roll(moved, 1, 1))
-        shown = jnp.where(lane == 0, 0.0, 1.0)
-        passed = jnp.where(lane == LANES - 1, 0.0, 1.0)
-        image = [pltpu.roll(h * shown, brick, 1) + pltpu.roll(r * passed, brick + 1, 1)
-                 for h, r in zip(here, right)]
-        image.append(pltpu.roll((1.0 - clear) * shown, brick, 1))
         through = run_ref[3, rows, :]
+        open_here = jnp.where(lane == brick, 0.0, through)
         for n in range(3):
-            run_ref[n, rows, :] = run_ref[n, rows, :] + through * image[n]
-        run_ref[3, rows, :] = through - through * image[3]
+            image = pltpu.roll(here[n], brick, 1) + pltpu.roll(right[n], brick + 1, 1)
+            run_ref[n, rows, :] = run_ref[n, rows, :] + open_here * image
+        run_ref[3, rows, :] = through - open_here * (1.0 - pltpu.roll(clear, brick, 1))
 
     def leave(first, last):
         leaving = (lane >= first) & (lane < last)

time: 59.8 us -> 60.7 us (1.015); the launches traced: 59.6 us -> 61.5 us
  blocking collectives: 46 us -> 47.4 us
    all_to_all x1, blocking collectives: 15.5 us -> 20.2 us  [body(): lax.all_to_all(merged.reshape(across * down, 1, -1), ('gx', 'gy'), 0, 0,...]
    all_to_all x1, blocking collectives: 30.5 us -> 27.2 us  [body(): swapped = lax.all_to_all(rows.reshape(depth, 1, -1), 'gz', 0, 0, tiled=True)]
  transfers between devices with their start and end apart: 1 -> 1, of which waited for: 0 -> 0; matrix products, arithmetic and copies ran while one was open for 0% -> 0% of each run, Pallas kernels for 8% -> 9%
where the time goes in v9:
time: 60.7 us; the launch traced here: 61.5 us
  blocking collectives  47.4 us (78%)
  Pallas kernels  8.55 us (14%)
  starting transfers between devices  3.95 us (7%)
  local copies, waits for them, and re-layouts  1.61 us (3%)
    all_to_all x1, blocking collectives, body(): swapped = lax.all_to_all(rows.reshape(depth, 1, -1), 'gz', 0, 0, tiled=True)  27.2 us
    all_to_all x1, blocking collectives, body(): lax.all_to_all(merged.reshape(across * down, 1, -1), ('gx', 'gy'), 0, 0,...  20.2 us
    pallas_call x1, Pallas kernels, render(): pl.pallas_call(render_kernel, in_specs=[pl.BlockSpec(memory_space=pltpu.S...  5.65 us
    ppermute x1, starting transfers between devices, body(): rim = lax.ppermute(last, 'gx', [(i, i + 1) for i in range(across - 1)])  3.95 us
    unnamed x10, local copies, waits for them, and re-layouts  1.61 us
  transfers between devices with their start and end apart: 1, of which 0 were waited for; matrix products, arithmetic and copies ran while one was open for 0% of the time, Pallas kernels for 9%

profile of v9, /device:TPU:1, one launch (start us, length us, event | category | flops | bytes accessed | tf_op | source)
XLA Modules:
  0.0 61.5 jit_solution(8210044710261759629)
XLA Ops:
  0.0 0.0 copy-start
  0.0 1.6 %copy-done = bf16[128,64,128]{2,1,0:T(8,128)(2,1)S(1)} copy-done((bf16[128,64,128]{2,1,0:T(8,128)(2,1)S(1)}, bf16[128,64,128]{2,1,0:T(8,128)(2,1)}, u32[]{:S(2)}) %copy-start) | copy-done | bytes 2097176
  1.6 0.0 copy-start.1
  1.6 0.0 copy-start.2
  1.6 0.0 copy-start.3
  1.6 0.0 copy-start.4
  1.6 0.6 %ends.1 = (f32[1,8192]{1,0:T(1,128)S(1)}, f32[1,8192]{1,0:T(1,128)S(1)}) custom-call(bf16[128,64,128]{2,1,0:T(8,128)(2,1)S(1)} %copy-done), custom_call_target="tpu_custom_call" | custom-call | tf_op jit(solution)/shard_map/ends/pallas_call | solution.py:317
  2.3 4.0 %collective-permute-start = (f32[64,128]{1,0:T(8,128)S(1)}, f32[64,128]{1,0:T(8,128)S(1)}, u32[]{:S(2)}, u32[]{:S(2)}) collective-permute-start(f32[64,128]{1,0:T(8,128)S(1)} %bitcast.21), channel_id=1, source_target_pairs={{0,128},{128,256},{256,384},{1,129},{129,257},{257,385},{2,130},{1... | collective-permute-start | bytes 98312 | tf_op jit(solution)/shard_map/ppermute | solution.py:333
  6.2 0.0 copy-done.1
  6.2 0.0 copy-done.2
  6.2 0.0 copy-done.3
  6.2 0.0 copy-done.4
  6.3 5.6 %render.1 = (f32[4,64,128]{2,1,0:T(8,128)S(1)}, f32[4,64,128]{2,1,0:T(8,128)S(1)}, f32[12,8,128]{2,1,0:T(8,128)S(1)}) custom-call(s32[16]{0:T(128)S(1)} %bitcast.19, f32[3,16]{1,0:T(4,128)S(1)} %copy-done.3, f32[1,16]{1,0:T(1,128)S(1)} %bitcast.15, bf16[128,64,128]{2,1,0:T(8,128)(2,1)S(1)} %copy-done.1), custom_call_target="tpu_custom_call" | custom-call | flops 40000000 | bytes 2400000 | tf_op jit(solution)/shard_map/render/pallas_call | solution.py:155
  11.9 0.0 collective-permute-done.rim_ref
  11.9 1.0 %deal.1 = s32[144,128]{1,0:T(8,128)S(1)} custom-call(s32[16]{0:T(128)S(1)} %bitcast.20, f32[12,8,128]{2,1,0:T(8,128)S(1)} %get-tuple-element.10.table_ref, f32[1,16]{1,0:T(1,128)S(1)} %bitcast.16, f32[64,128]{1,0:T(8,128)S(1)} %bitcast.14, f32[64,128]{1,0:T(8,128)S(1)} %collective-permute-done.rim_ref, f32[4,64,128]{2,1,0:T(8,128)S(1)} %get-tuple-element.13.run_ref, ...), custom_call_target="tpu_custom_call" | custom-call | tf_op jit(solution)/shard_map/deal/pallas_call | solution.py:220
  12.9 27.2 %all_to_all.10 = s32[16,1,1152]{2,1,0:T(1,128)S(1)} all-to-all(s32[16,1,1152]{2,1,0:T(1,128)S(1)} %bitcast.10), channel_id=1, replica_groups=mesh['gx'=4,'gy'=8,'gz'=16] {'gz'}, dimensions={0} | all-to-all | bytes 147456 | tf_op jit(solution)/shard_map/all_to_all | solution.py:336
  40.1 0.3 along_depth.1
  40.4 20.2 %all_to_all.11 = s32[32,1,128]{2,1,0:T(1,128)S(1)} all-to-all(s32[32,1,128]{2,1,0:T(1,128)S(1)} %bitcast.13), channel_id=1, replica_groups=mesh['gx'=4,'gy'=8,'gz'=16] {'gx','gy'}, dimensions={0} | all-to-all | bytes 32768 | tf_op jit(solution)/shard_map/all_to_all | solution.py:338
  60.6 1.0 %gather.1 = f32[4,1,768]{2,1,0:T(1,128)} custom-call(f32[1,16]{1,0:T(1,128)S(1)} %bitcast.18, s32[32,128]{1,0:T(8,128)S(1)} %bitcast.12), custom_call_target="tpu_custom_call" | custom-call | tf_op jit(solution)/shard_map/gather/pallas_call | solution.py:293
Async XLA Ops:
  0.0 1.6 %copy-start = (bf16[128,64,128]{2,1,0:T(8,128)(2,1)S(1)}, bf16[128,64,128]{2,1,0:T(8,128)(2,1)}, u32[]{:S(2)}) copy-start(bf16[128,64,128]{2,1,0:T(8,128)(2,1)} %volume_ref.3) | copy-start | bytes 6291460
  1.6 4.6 %copy-start.1 = (bf16[128,64,128]{2,1,0:T(8,128)(2,1)S(1)}, bf16[128,64,128]{2,1,0:T(8,128)(2,1)}, u32[]{:S(2)}) copy-start(bf16[128,64,128]{2,1,0:T(8,128)(2,1)} %volume_ref.3) | copy-start | bytes 6291460
  1.6 4.6 %copy-start.2 = (f32[16]{0:T(128)S(1)}, f32[16]{0:T(128)}, u32[]{:S(2)}) copy-start(f32[16]{0:T(128)} %param.6) | copy-start | bytes 196
  1.6 4.6 %copy-start.3 = (f32[3,16]{1,0:T(4,128)S(1)}, f32[3,16]{1,0:T(4,128)}, u32[]{:S(2)}) copy-start(f32[3,16]{1,0:T(4,128)} %color_ref.1) | copy-start | bytes 580
  1.6 4.6 %copy-start.4 = (s32[16,1,1]{0,2,1:T(1,128)S(1)}, s32[16,1,1]{0,2,1:T(1,128)}, u32[]{:S(2)}) copy-start(s32[16,1,1]{0,2,1:T(1,128)} %param.7) | copy-start | bytes 196
  2.3 9.7 %collective-permute-start = (f32[64,128]{1,0:T(8,128)S(1)}, f32[64,128]{1,0:T(8,128)S(1)}, u32[]{:S(2)}, u32[]{:S(2)}) collective-permute-start(f32[64,128]{1,0:T(8,128)S(1)} %bitcast.21), channel_id=1, source_target_pairs={{0,128},{128,256},{256,384},{1,129},{129,257},{257,385},{2,130},{1... | collective-permute-start | bytes 98312 | tf_op jit(solution)/shard_map/ppermute | solution.py:333
